TPU v7x, 32 devices: a whole 2x2x4 slice. The times are simulated.
32 devices in a mesh: groups: 2 (over y), wide: 4 (over z), narrow: 4 (over x, core).
Axes of the slice: x: 2, y: 2, z: 4, core: 2. Of those that a mesh axis runs over, the one named last changes fastest.
Arguments:
- hidden: bfloat16 [96, 8192], P(('groups', 'wide')), parts along dimension 0, may hold values from -6 to 6
- attention_norm_gain: bfloat16 [8192], replicated, may hold values from 0.5 to 1.5
- row_adapter_index: int32 [96], P(('groups', 'wide')), parts along dimension 0, may hold values from 0 to 31
- lengths: int32 [96], P(('groups', 'wide')), parts along dimension 0, may hold values from 1 to 192, as said below
- paged_key_cache: bfloat16 [96, 8, 192, 128], P(('groups', 'wide'), 'narrow'), parts along dimension 0, may hold values from -510 to 510
- paged_value_cache: bfloat16 [96, 8, 192, 128], P(('groups', 'wide'), 'narrow'), parts along dimension 0, may hold values from -6 to 6
- query_weight: bfloat16 [8192, 8192], P('wide', 'narrow'), may hold values from -0.0625 to 0.0625
- key_weight: bfloat16 [8192, 1024], P('wide', 'narrow'), may hold values from -0.0625 to 0.0625
- value_weight: bfloat16 [8192, 1024], P('wide', 'narrow'), may hold values from -0.0625 to 0.0625
- adapter_down_weight: bfloat16 [64, 3, 64, 8192], P(('groups', 'wide'), None, None, 'narrow'), parts along dimension 0, may hold values from -0.0625 to 0.0625
- adapter_up_query: bfloat16 [64, 64, 8192], P(('groups', 'wide'), None, 'narrow'), parts along dimension 0, may hold values from -0.75 to 0.75
- adapter_up_key_value: bfloat16 [64, 2, 64, 1024], P(('groups', 'wide'), None, None, 'narrow'), parts along dimension 0, may hold values from -0.75 to 0.75
Outputs:
- attention: bfloat16 [96, 8192], P(('groups', 'wide'), 'narrow'), parts along dimension 0
There are 2 independent parts, one for each index of `groups`. A program takes and returns all parts, laid end to end along the dimension named above; an argument that names none is the same for every part. Nothing has to cross between parts.
Inputs may be any that keep to these rules, and one draw needn't show every extreme that they name: Row r's cache holds keys and values at positions 0 to lengths[r] - 1; some row has all 192.
All inputs are finite; a program needn't handle non-finite values.
Results may differ from a plain program's by a relative error of at most 0.008.
The roundings to bfloat16 on the way count: a program that leaves them out, or rounds other values in their place, can miss the bound.
Values may be sent and summed in bfloat16 or wider, within the bound.
No kernel may reach another device: no remote copies, remote signals or barrier semaphores. Data moves between devices by JAX's collectives and lax.ppermute only.
A program may use at most 64 MiB of HBM per device.

v0:
```python
import math

import jax
import jax.numpy as jnp
from jax import lax
from jax.sharding import PartitionSpec as P

HEAD_WIDTH = 128


adapter_scale = 0.5
rope_base = 500000.0
epsilon = 1e-05


def normalize(hidden, attention_norm_gain):
    values = hidden.astype(jnp.float32)
    factor = lax.rsqrt(jnp.mean(values * values, axis=-1, keepdims=True) + epsilon)
    return (values * factor * attention_norm_gain.astype(jnp.float32)[None, :]).astype(jnp.bfloat16)


def rotate(vectors, positions):
    half_dim = vectors.shape[-1] // 2
    frequency = rope_base ** (-2.0 * jnp.arange(half_dim, dtype=jnp.float32) / vectors.shape[-1])
    angles = positions.astype(jnp.float32)[:, None] * frequency[None, :]
    cosine = jnp.cos(angles)[:, None, :]
    sine_part = jnp.sin(angles)[:, None, :]
    lower_half = vectors[..., :half_dim]
    upper_half = vectors[..., half_dim:]
    return jnp.concatenate(
        [
            lower_half * cosine - upper_half * sine_part,
            upper_half * cosine + lower_half * sine_part,
        ],
        axis=-1,
    )


def attend(queries, new_keys, new_values, paged_key_cache, paged_value_cache, lengths):
    factor = 1.0 / math.sqrt(queries.shape[-1])
    scores = (
        jnp.einsum("rgqd,rgld->rgql", queries, paged_key_cache, preferred_element_type=jnp.float32)
        * factor
    )
    own_score = (
        jnp.einsum("rgqd,rgd->rgq", queries, new_keys, preferred_element_type=jnp.float32) * factor
    )
    visible = (
        jnp.arange(paged_key_cache.shape[2], dtype=jnp.int32)[None, None, None, :]
        < lengths[:, None, None, None]
    )
    scores = jnp.where(visible, scores, -jnp.inf)
    row_max = jnp.maximum(jnp.max(scores, axis=-1), own_score)
    weights = jnp.exp(scores - row_max[..., None])
    own_weight = jnp.exp(own_score - row_max)
    denominator = jnp.sum(weights, axis=-1) + own_weight
    weights = (weights / denominator[..., None]).astype(jnp.bfloat16)
    own_weight = (own_weight / denominator).astype(jnp.bfloat16)
    attended = jnp.einsum(
        "rgql,rgld->rgqd", weights, paged_value_cache, preferred_element_type=jnp.float32
    )
    attended = (
        attended
        + own_weight.astype(jnp.float32)[..., None] * new_values.astype(jnp.float32)[:, :, None, :]
    )
    return attended.astype(jnp.bfloat16)


def on_device(
    hidden,
    attention_norm_gain,
    row_adapter_index,
    lengths,
    paged_key_cache,
    paged_value_cache,
    query_weight,
    key_weight,
    value_weight,
    adapter_down_weight,
    adapter_up_query,
    adapter_up_key_value,
):
    rows_dev = hidden.shape[0]
    narrow = lax.axis_size("narrow")
    normed = normalize(hidden, attention_norm_gain)
    feature_cols = lax.all_to_all(normed, "wide", split_axis=1, concat_axis=0, tiled=True)
    portion_width = normed.shape[1] // narrow
    my_slice = lax.dynamic_slice_in_dim(
        normed, lax.axis_index("narrow") * portion_width, portion_width, 1
    )
    gathered, row_adapter = (
        lax.all_gather(my_slice, "wide", axis=0, tiled=True),
        lax.all_gather(row_adapter_index, "wide", axis=0, tiled=True),
    )
    per_shard_count = adapter_down_weight.shape[0]
    adapter_rank_size = adapter_down_weight.shape[2]
    local_index = row_adapter - lax.axis_index("wide") * per_shard_count
    select = local_index[:, None] == jnp.arange(per_shard_count, dtype=jnp.int32)[None, :]
    flattened_down_weight = adapter_down_weight.reshape(
        per_shard_count * 3 * adapter_rank_size, portion_width
    )
    value_partial_sums = lax.dot_general(
        gathered,
        flattened_down_weight,
        (((1,), (1,)), ((), ())),
        preferred_element_type=jnp.float32,
    )
    value_partial_sums = value_partial_sums.reshape(
        value_partial_sums.shape[0], per_shard_count, 3 * adapter_rank_size
    )
    value_partial_sums = jnp.sum(jnp.where(select[:, :, None], value_partial_sums, 0.0), axis=1)
    rank_sums = lax.psum(value_partial_sums, "narrow").astype(jnp.bfloat16)
    chosen = select.astype(jnp.bfloat16)

    def widen_rows(adapter_products):
        return (chosen[:, :, None] * adapter_products[:, None, :]).reshape(
            adapter_products.shape[0], per_shard_count * adapter_rank_size
        )

    query_update = jnp.dot(
        widen_rows(rank_sums[:, :adapter_rank_size]),
        adapter_up_query.reshape(per_shard_count * adapter_rank_size, -1),
        preferred_element_type=jnp.float32,
    )
    key_update = jnp.dot(
        widen_rows(rank_sums[:, adapter_rank_size : 2 * adapter_rank_size]),
        adapter_up_key_value[:, 0].reshape(per_shard_count * adapter_rank_size, -1),
        preferred_element_type=jnp.float32,
    )
    value_update = jnp.dot(
        widen_rows(rank_sums[:, 2 * adapter_rank_size :]),
        adapter_up_key_value[:, 1].reshape(per_shard_count * adapter_rank_size, -1),
        preferred_element_type=jnp.float32,
    )
    adapter_updates = adapter_scale * jnp.concatenate(
        [query_update, key_update, value_update], axis=1
    )
    base_part = lax.psum_scatter(
        jnp.concatenate(
            [
                jnp.dot(feature_cols, matrix, preferred_element_type=jnp.float32)
                for matrix in (query_weight, key_weight, value_weight)
            ],
            axis=1,
        ),
        "wide",
        scatter_dimension=0,
        tiled=True,
    )
    projected_rows = base_part + lax.psum_scatter(
        adapter_updates, "wide", scatter_dimension=0, tiled=True
    )
    query_width = query_weight.shape[1]
    kv_width = key_weight.shape[1]
    head_count = query_width // HEAD_WIDTH
    kv_heads = kv_width // HEAD_WIDTH
    queries = rotate(
        projected_rows[:, :query_width].reshape(rows_dev, head_count, HEAD_WIDTH), lengths
    ).astype(jnp.bfloat16)
    new_keys = rotate(
        projected_rows[:, query_width : query_width + kv_width].reshape(
            rows_dev, kv_heads, HEAD_WIDTH
        ),
        lengths,
    ).astype(jnp.bfloat16)
    new_values = (
        projected_rows[:, query_width + kv_width :]
        .reshape(rows_dev, kv_heads, HEAD_WIDTH)
        .astype(jnp.bfloat16)
    )
    grouped = queries.reshape(rows_dev, kv_heads, head_count // kv_heads, HEAD_WIDTH)
    attended = attend(grouped, new_keys, new_values, paged_key_cache, paged_value_cache, lengths)
    return attended.reshape(rows_dev, query_width)


def solution(mesh):
    in_specs = (
        P(("groups", "wide"), None),
        P(),
        P(("groups", "wide")),
        P(("groups", "wide")),
        P(("groups", "wide"), "narrow", None, None),
        P(("groups", "wide"), "narrow", None, None),
        P("wide", "narrow"),
        P("wide", "narrow"),
        P("wide", "narrow"),
        P(("groups", "wide"), None, None, "narrow"),
        P(("groups", "wide"), None, "narrow"),
        P(("groups", "wide"), None, None, "narrow"),
    )
    out_specs = P(("groups", "wide"), "narrow")
    return jax.shard_map(
        on_device, mesh=mesh, in_specs=in_specs, out_specs=out_specs, check_vma=False
    )
```

profile of v0, /device:TPU:0, one launch (start us, length us, event | category | flops | bytes accessed | tf_op | source)
XLA Modules:
  0.0 120.9 jit_solution(15049287755094513651)
XLA Ops:
  6.5 0.9 convert_element_type.55
  7.4 1.1 fusion.4
  8.5 1.1 fusion.6
  9.6 0.1 all_to_all.14
  9.8 0.8 copy.16
  10.6 6.3 %all-to-all-start = ((bf16[12,4,2048]{2,0,1:T(8,128)(2,1)}), bf16[12,4,2048]{2,0,1:T(8,128)(2,1)S(1)}, u32[]{:S(2)}, u32[]{:S(2)}) async-start(bf16[12,4,2048]{2,0,1:T(8,128)(2,1)} %copy.16), calls=%async_computation | async-start | bytes 524288 | tf_op jit(solution)/shard_map/all_to_all | solution.py:86
  16.9 17.5 %all-gather = bf16[4,12,2048]{2,1,0:T(8,128)(2,1)S(1)} all-gather(bf16[1,12,2048]{2,1,0:T(8,128)(2,1)S(1)} %dynamic-slice_bitcast_fusion), channel_id=1, replica_groups=mesh['groups'=2,'wide'=4,'narrow'=4] {'wide'}, dimensions={0}, use_global_device_ids=true | all-gather | bytes 245760 | tf_op jit(solution)/shard_map/all_gather | solution.py:92
  34.5 0.7 fusion.23
  35.9 0.2 dynamic-update-slice
  36.1 6.5 %all-reduce = s32[48]{0:T(128)S(1)} all-reduce(s32[48]{0:T(128)S(1)} %dynamic-update-slice), channel_id=1, replica_groups=mesh['groups'=2,'wide'=4,'narrow'=4] {'wide'}, use_global_device_ids=true, to_apply=%add | all-reduce | flops 48 | bytes 384
  42.7 4.9 %fusion = f32[48,192]{1,0:T(8,128)S(1)} fusion(bf16[48,2048,1]{1,0,2:T(8,128)(2,1)S(1)} %reshape.195, bf16[8,192,2048]{2,1,0:T(8,128)(2,1)} %bitcast.41, pred[48,8]{0,1:T(8,128)(4,1)S(1)} %get-tuple-element.24), kind=kOutput, calls=%fused_computation.2 | convolution fusion | flops 302128128 | bytes 6525312 | tf_op jit(solution)/shard_map/dot_general | solution.py:102
  47.6 10.5 %psum.7 = bf16[48,192]{1,0:T(8,128)(2,1)S(1)} all-reduce(f32[48,192]{1,0:T(8,128)S(1)} %fusion), channel_id=1, replica_groups=mesh['groups'=2,'wide'=4,'narrow'=4] {'narrow'}, use_global_device_ids=true, to_apply=%region_3.4 | all-reduce | flops 9216 | bytes 55296 | tf_op jit(solution)/shard_map/psum | solution.py:112
  58.3 0.8 broadcast_multiply_fusion.2
  59.1 0.1 mul.209
  59.3 0.2 fusion.28
  59.5 1.4 %convolution_bitcast_fusion = f32[48,2048]{1,0:T(8,128)S(1)} fusion(bf16[8,64,2048]{2,1,0:T(8,128)(2,1)S(1)} %copy-done, bf16[48,8,64]{2,1,0:T(8,128)(2,1)} %get-tuple-element.16), kind=kOutput, calls=%fused_computation | convolution fusion | flops 100663296 | bytes 2539520 | tf_op jit(solution)/shard_map/dot_general | solution.py:120
  60.9 0.1 mul.212
  61.0 0.2 fusion.29
  61.3 5.1 %fusion.25 = f32[48,2048]{1,0:T(8,128)S(1)} fusion(bf16[48,2048]{1,0:T(8,128)(2,1)S(1)} %all_to_all.17, bf16[2048,2048]{1,0:T(8,128)(2,1)} %param.18), kind=kOutput, calls=%fused_computation.57 | convolution fusion | flops 402653184 | bytes 8978432 | tf_op jit(solution)/shard_map/dot_general | solution.py:141
  66.4 0.3 fusion.26
  66.7 0.3 fusion.27
  67.0 0.9 maximum_add_fusion
  68.7 0.1 multiply_cosine_fusion
  68.8 37.3 %all-reduce.4.cloned.1.call-done = f32[48,2560]{1,0:T(8,128)} async-done(((f32[48,2560]{1,0:T(8,128)}), f32[48,2560]{1,0:T(8,128)}) %all-reduce.4.cloned.1.call-update) | async-done | bytes 491536
  106.1 0.8 dynamic-slice.4
  107.0 0.9 constant_dynamic-slice_fusion
  108.2 0.2 fusion.13
  108.4 2.1 %fusion.24 = (f32[12,2,8]{2,1,0:T(2,128)S(1)}, f32[12,2,8,192]{3,2,1,0:T(8,128)S(1)}) fusion(bf16[12,2,192,128]{3,2,1,0:T(8,128)(2,1)} %param.16, bf16[12,2,8,64]{3,2,1,0:T(8,128)(2,1)S(1)} %get-tuple-element.8, bf16[12,2,8,64]{3,2,1,0:T(8,128)(2,1)S(1)} %get-tuple-element.7, pred[12,192]{1,0:T(8,128)(4,1)S(1)} %iota_compare_fusion), kind=kOutput, calls=%fused_computation.56 | convolution fusion | flops 9645888 | bytes 1379328 | tf_op jit(solution)/shard_map/rgqd,rgld->rgql/dot_general | solution.py:42
  110.6 0.2 fusion.7
  110.8 0.8 fusion.15
  111.7 1.7 %fusion.3 = bf16[12,16,128]{2,1,0:T(8,128)(2,1)S(1)} fusion(bf16[12,2,192,128]{3,2,1,0:T(8,128)(2,1)} %param.17, f32[12,2,8,192]{3,2,1,0:T(8,128)S(1)} %get-tuple-element.26, f32[12,2,8]{2,1,0:T(2,128)S(1)} %get-tuple-element.10, f32[12,2,8]{2,1,0:T(2,128)S(1)} %multiply_maximum_fusion, f32[12,2,128]{2,1,0:T(2,128)S(1)} %reshape.187, ...), kind=kOutput, calls=%fused_computation.7 | convolution fusion | flops 9621504 | bytes 1390848 | tf_op jit(solution)/shard_map/rgql,rgld->rgqd/dot_general | solution.py:59
  113.4 0.6 copy.22
  (42 shorter events, 0.9 us)
Async XLA Ops:
  6.5 52.9 %copy-start = (bf16[8,64,2048]{2,1,0:T(8,128)(2,1)S(1)}, bf16[8,64,2048]{2,1,0:T(8,128)(2,1)}, u32[]{:S(2)}) copy-start(bf16[8,64,2048]{2,1,0:T(8,128)(2,1)} %param.22) | copy-start | bytes 6291460
  6.5 28.0 %copy-start.5 = (u32[32]{0:T(128)S(1)}, u32[32]{0:T(128)}, u32[]{:S(2)}) copy-start(u32[32]{0:T(128)} %constant.43) | copy-start | bytes 388
  6.5 29.4 %copy-start.7 = (s32[12]{0:T(128)S(1)}, s32[12]{0:T(128)}, u32[]{:S(2)}) copy-start(s32[12]{0:T(128)} %param.14) | copy-start | bytes 148
  10.6 50.6 %all-to-all-start = ((bf16[12,4,2048]{2,0,1:T(8,128)(2,1)}), bf16[12,4,2048]{2,0,1:T(8,128)(2,1)S(1)}, u32[]{:S(2)}, u32[]{:S(2)}) async-start(bf16[12,4,2048]{2,0,1:T(8,128)(2,1)} %copy.16), calls=%async_computation | async-start | bytes 524288 | tf_op jit(solution)/shard_map/all_to_all | solution.py:86
  16.9 89.2 %all-reduce.4.cloned.1.call-start = ((), (), s32[]{:S(2)}) async-start(), calls=%async_computation.1 | async-start | bytes 983040
  42.7 16.6 %copy-start.3 = (bf16[8,2,64,256]{3,2,1,0:T(8,128)(2,1)S(1)}, bf16[8,2,64,256]{3,2,1,0:T(8,128)(2,1)}, u32[]{:S(2)}) copy-start(bf16[8,2,64,256]{3,2,1,0:T(8,128)(2,1)} %param.23) | copy-start | bytes 1572868
  59.3 1.6 %copy-start.4 = (bf16[48,8,64]{2,1,0:T(8,128)(2,1)S(1)}, bf16[48,8,64]{2,1,0:T(8,128)(2,1)}, u32[]{:S(2)}) copy-start(bf16[48,8,64]{2,1,0:T(8,128)(2,1)} %get-tuple-element.18) | copy-start | bytes 147460
  61.3 5.1 %copy-start.1 = (bf16[2048,256]{1,0:T(8,128)(2,1)S(1)}, bf16[2048,256]{1,0:T(8,128)(2,1)}, u32[]{:S(2)}) copy-start(bf16[2048,256]{1,0:T(8,128)(2,1)} %param.19) | copy-start | bytes 3145732
  61.3 5.4 %copy-start.2 = (bf16[2048,256]{1,0:T(8,128)(2,1)S(1)}, bf16[2048,256]{1,0:T(8,128)(2,1)}, u32[]{:S(2)}) copy-start(bf16[2048,256]{1,0:T(8,128)(2,1)} %param.20) | copy-start | bytes 3145732
  66.4 1.5 %copy-start.6 = (s32[12]{0:T(128)S(1)}, s32[12]{0:T(128)}, u32[]{:S(2)}) copy-start(s32[12]{0:T(128)} %param.15) | copy-start | bytes 148
Sparse Core Ops, SparseCore 0:
  68.0 38.0 all-reduce.3
where the time goes:
time: 121 us
  waiting for transfers between devices  37.3 us (31%)
  blocking collectives  34.5 us (29%)
  matrix products  16.4 us (14%)
  between operations  15 us (12%)
  other arithmetic  6.35 us (5%)
  starting transfers between devices  6.32 us (5%)
  local copies, waits for them, and re-layouts  4.98 us (4%)
    unnamed x2, waiting for transfers between devices  37.3 us
    all_gather x1, blocking collectives, on_device(): lax.all_gather(my_slice, 'wide', axis=0, tiled=True)  17.5 us
    psum x1, blocking collectives, on_device(): rank_sums = lax.psum(value_partial_sums, 'narrow').astype(jnp.bfloat16)  10.5 us
    unnamed x1, blocking collectives  6.5 us
    all_to_all x1, starting transfers between devices, on_device(): lax.all_to_all(normed, 'wide', split_axis=1, concat_axis=0, tiled=True)  6.32 us
    dot_general x3, matrix products, on_device(): jnp.dot(feature_cols, matrix, preferred_element_type=jnp.float32)  5.68 us
    dot_general x1, matrix products, on_device(): lax.dot_general(gathered, flattened_down_weight, (((1,), (1,)), ((), ()))...  4.94 us
  transfers between devices with their start and end apart: 2, of which 1 were waited for; matrix products, arithmetic and copies ran while one was open for 8% of the time, Pallas kernels for 0%

commit v1 on v0

v1 whole, which is shorter than its diff:
```python
import functools
import math

import jax
import jax.numpy as jnp
from jax import lax
from jax.experimental import pallas as pl
from jax.experimental.pallas import tpu as pltpu
from jax.sharding import PartitionSpec as P

HEAD_WIDTH = 128
LANES = 128

adapter_scale = 0.5
rope_base = 500000.0
epsilon = 1e-05

RING = (0, 1, 2, 3)
XOR = False
N_ORDER = (1, 2, 3)
W_ORDER = (1, 2, 3)
O_ORDER = (2, 1, 3)

f32 = jnp.float32
bf16 = jnp.bfloat16

VMEM = pl.BlockSpec(memory_space=pltpu.VMEM)
ANY = pl.BlockSpec(memory_space=pl.ANY)
HBM = pl.BlockSpec(memory_space=pltpu.HBM)


def shape_of(shape, dtype):
    return jax.ShapeDtypeStruct(shape, dtype)


def call(kernel, outs, in_specs, args, scratch=(), flops=0, nbytes=0, vmem=8):
    return pl.pallas_call(
        kernel,
        out_shape=outs,
        in_specs=in_specs,
        out_specs=jax.tree.map(lambda _: VMEM, outs),
        scratch_shapes=scratch,
        compiler_params=pltpu.CompilerParams(vmem_limit_bytes=vmem * 2**20),
        cost_estimate=pl.CostEstimate(flops=flops, bytes_accessed=nbytes, transcendentals=0),
    )(*args)


def own_place():
    return lax.axis_index("wide"), lax.axis_index("narrow")


def normalize_kernel(wide, index_far, hidden_far, gain_far, message, *refs):
    slices, (scratch, index, hidden, gain, sems) = refs[:wide], refs[wide:]
    copies = [
        pltpu.make_async_copy(far, near, sems.at[i])
        for i, (far, near) in enumerate(
            ((hidden_far, hidden), (gain_far, gain), (index_far, index))
        )
    ]
    for copy in copies:
        copy.start()
    wide_place, narrow_place = own_place()
    rows = hidden.shape[0]
    half = message.shape[1] - LANES
    wide_half = slices[0].shape[1]
    copies[0].wait()
    values = hidden[...].astype(f32)
    factor = lax.rsqrt(jnp.mean(values * values, axis=-1, keepdims=True) + epsilon)
    copies[1].wait()
    copies[2].wait()
    scale = gain[...].astype(f32).reshape(1, -1)
    normed = (values * factor * scale).astype(bf16)
    scratch[...] = normed.astype(f32)

    def stacked(start, width):
        return jnp.concatenate(
            [
                scratch[:, pl.ds(pl.multiple_of(start, LANES), width)],
                scratch[:, pl.ds(pl.multiple_of(start + width, LANES), width)],
            ],
            axis=0,
        ).astype(bf16)

    message[:, :half] = stacked(narrow_place * (2 * half), half)
    row = lax.broadcasted_iota(jnp.int32, (2 * rows, LANES), 0)
    ids = jnp.zeros((2 * rows, LANES), f32)
    for r in range(rows):
        ids = jnp.where((row == r) | (row == r + rows), index[r].astype(f32), ids)
    message[:, half:] = ids.astype(bf16)
    for k in range(wide):
        target = after(wide_place, k, wide)
        slices[k][...] = stacked(target * (2 * wide_half), wide_half)


def joined(blocks):
    rows = blocks[0].shape[0] // 2
    values = [block[...].astype(f32) for block in blocks]
    upper = jnp.concatenate([value[:rows] for value in values], axis=0)
    lower = jnp.concatenate([value[rows:] for value in values], axis=0)
    return upper, lower


def down_kernel(wide, rank3, *refs):
    blocks, down, (sums, ids) = refs[:wide], refs[wide], refs[wide + 1 :]
    wide_place, _ = own_place()
    count = down.shape[0] // rank3
    upper, lower = joined(restored(blocks, N_ORDER))
    half = upper.shape[1] - LANES
    row_ids = upper[:, half:]
    ids[...] = row_ids
    features = jnp.concatenate([upper[:, :half], lower[:, :half]], axis=1).astype(bf16)
    first = wide_place * count
    total = jnp.zeros((features.shape[0], rank3), f32)
    for e in range(count):
        product = lax.dot_general(
            features,
            down[e * rank3 : (e + 1) * rank3, :],
            (((1,), (1,)), ((), ())),
            preferred_element_type=f32,
        )
        total = jnp.where(row_ids[:, :1] == (first + e).astype(f32), product, total)
    sums[...] = total


def base_kernel(wide, *refs):
    blocks, sources, out = refs[:wide], refs[wide:-1], refs[-1]
    chunk = 256
    upper, lower = (part.astype(bf16) for part in joined(restored(blocks, W_ORDER)))
    half = upper.shape[1]
    offset = 0
    for source in sources:
        for start in range(0, source.shape[1], chunk):
            columns = slice(start, start + chunk)
            out[:, offset + start : offset + start + chunk] = jnp.dot(
                upper, source[:half, columns], preferred_element_type=f32
            ) + jnp.dot(lower, source[half:, columns], preferred_element_type=f32)
        offset += source.shape[1]


LARGEST = 32767.0
STEP_ROWS = 16


def step_of(exponent):
    return jnp.exp2(exponent * 0.25) * (1.0 / LARGEST)


def up_kernel(wide, narrow, base, ids, *refs):
    parts, (query_up, pair_up) = refs[:narrow], refs[narrow : narrow + 2]
    own, *outs = refs[narrow + 2 : narrow + 2 + wide]
    sums, codes = refs[narrow + 2 + wide :]
    wide_place, _ = own_place()
    count, _, rank, pair_width = pair_up.shape
    all_rows, width = base.shape
    rows = all_rows // wide
    total = parts[0][...]
    for part in parts[1:]:
        total = total + part[...]
    rank_sums = total.astype(bf16)
    row_ids = ids[:, :1]
    first = wide_place * count

    def widen(p):
        piece = rank_sums[:, p * rank : (p + 1) * rank].astype(f32)
        return jnp.concatenate(
            [jnp.where(row_ids == (first + e).astype(f32), piece, 0.0) for e in range(count)],
            axis=1,
        ).astype(bf16)

    chunk = 256
    query_width = query_up.shape[1]
    pairs = [
        jnp.concatenate([pair_up[e, p] for e in range(count)], axis=0) for p in range(2)
    ]
    groups = (
        (widen(0), query_up, 0, query_width),
        (widen(1), pairs[0], query_width, pair_width),
        (widen(2), pairs[1], query_width + pair_width, pair_width),
    )
    exponents = []
    for lhs, weights, offset, group_width in groups:
        top = jnp.zeros((all_rows, LANES), f32)
        for start in range(0, group_width, chunk):
            columns = slice(offset + start, offset + start + chunk)
            values = base[:, columns] + adapter_scale * jnp.dot(
                lhs, weights[:, start : start + chunk], preferred_element_type=f32
            )
            sums[:, columns] = values
            for j in range(0, chunk, LANES):
                top = jnp.maximum(top, jnp.abs(values[:, j : j + LANES]))
        top = jnp.maximum(jnp.max(top, axis=-1, keepdims=True), 1e-30)
        exponents.append(jnp.ceil(4.0 * jnp.log2(top) + 0.01))
    for (_, _, offset, group_width), exponent in zip(groups, exponents):
        inverse = 1.0 / step_of(exponent)
        for start in range(offset, offset + group_width, LANES):
            values = sums[:, start : start + LANES]
            window = slice(start // LANES * rows, (start // LANES + 1) * rows)
            own[window, :] = values[:rows]
            rounded = jnp.round(values * inverse)
            for k in range(1, wide):
                codes[k - 1, window, :] = rounded[k * rows : (k + 1) * rows]
    lane = lax.broadcasted_iota(jnp.int32, (all_rows, LANES), 1)
    marks = jnp.where(
        lane < 32, exponents[0], jnp.where(lane < 64, exponents[1], exponents[2])
    )
    body = width // LANES * rows
    rest = jnp.zeros((outs[0].shape[0] - body - rows, LANES), f32)
    for k in range(1, wide):
        mark = jnp.concatenate([marks[k * rows : (k + 1) * rows], rest], axis=0)
        outs[k - 1][:body, :] = codes[k - 1].astype(jnp.int32).astype(jnp.int16)
        outs[k - 1][body:, :] = mark.astype(jnp.int32).astype(jnp.int16)


def attend_kernel(wide, heads, kv_heads, visible, cosine, sine, *refs):
    parts, (keys, values, out, rotated, attended) = refs[:wide], refs[wide:]
    rows, _, _, width = keys.shape
    group = heads // kv_heads
    body = (heads + 2 * kv_heads) * rows
    total = parts[0][...]
    for part in parts[1:]:
        steps = step_of(part[body:, :].astype(jnp.int32).astype(f32)[:rows])
        query_step, key_step, value_step = (
            jnp.broadcast_to(steps[:, lane : lane + 1], (rows, width)) for lane in (0, 32, 64)
        )
        step = jnp.concatenate(
            [query_step] * heads + [key_step] * kv_heads + [value_step] * kv_heads, axis=0
        )
        total = total + part[:body, :].astype(jnp.int32).astype(f32) * step
    turned = (heads + kv_heads) * rows
    straight = total[:turned]
    straight = straight * cosine[...] + pltpu.roll(straight, width // 2, 1) * sine[...]
    rotated[:turned] = straight.astype(bf16).astype(f32)
    rotated[turned:] = total[turned:].astype(bf16).astype(f32)
    factor = 1.0 / math.sqrt(width)
    pairs = [(r, g) for r in range(rows) for g in range(kv_heads)]
    scores, own = [], []
    for r, g in pairs:
        query = rotated[pl.ds(g * group * rows + r, group, stride=rows), :]
        new_key = rotated[pl.ds((heads + g) * rows + r, 1), :]
        score = lax.dot_general(
            query.astype(bf16), keys[r, g], (((1,), (1,)), ((), ())), preferred_element_type=f32
        )
        scores.append(score * factor + visible[r : r + 1, :])
        own.append(jnp.sum(query * new_key, axis=-1, keepdims=True) * factor)
    score, own = jnp.concatenate(scores, axis=0), jnp.concatenate(own, axis=0)
    row_max = jnp.maximum(jnp.max(score, axis=-1, keepdims=True), own)
    weights = jnp.exp(score - row_max)
    own_weight = jnp.exp(own - row_max)
    denominator = jnp.sum(weights, axis=-1, keepdims=True) + own_weight
    weights = (weights / denominator).astype(bf16)
    own_weight = (own_weight / denominator).astype(bf16).astype(f32)
    mixed = []
    for i, (r, g) in enumerate(pairs):
        new_value = rotated[pl.ds((heads + kv_heads + g) * rows + r, 1), :]
        window = slice(i * group, (i + 1) * group)
        mixed.append(
            jnp.dot(weights[window], values[r, g], preferred_element_type=f32)
            + own_weight[window] * new_value
        )
    for i, (r, g) in enumerate(pairs):
        attended[pl.ds(g * group * rows + r, group, stride=rows), :] = mixed[i]
    for h in range(heads):
        out[:, h * width : (h + 1) * width] = attended[h * rows : (h + 1) * rows, :].astype(bf16)


def rotation_kernel(lengths_far, after, cosine, sine, visible, lengths, sem):
    copy = pltpu.make_async_copy(lengths_far, lengths, sem)
    copy.start()
    rows, positions = visible.shape
    half_dim = HEAD_WIDTH // 2
    lane = lax.broadcasted_iota(jnp.int32, (rows, HEAD_WIDTH), 1)
    place = jnp.where(lane < half_dim, lane, lane - half_dim).astype(f32)
    frequency = jnp.exp(place * (-2.0 / HEAD_WIDTH * math.log(rope_base)))
    row = lax.broadcasted_iota(jnp.int32, (rows, positions), 0)
    length = jnp.zeros((rows, positions), jnp.int32)
    copy.wait()
    for r in range(rows):
        length = jnp.where(row == r, lengths[r], length)
    position = lax.broadcasted_iota(jnp.int32, (rows, positions), 1)
    visible[...] = jnp.where(position < length, 0.0, -jnp.inf)
    angles = length[:, :HEAD_WIDTH].astype(f32) * frequency
    cosines = jnp.cos(angles)
    sines = jnp.where(lane < half_dim, -1.0, 1.0) * jnp.sin(angles)
    repeats = cosine.shape[0] // rows
    cosine[...] = jnp.concatenate([cosines] * repeats, axis=0)
    sine[...] = jnp.concatenate([sines] * repeats, axis=0)


def arranged(order, count):
    return [k for k in order if k < count] + [k for k in range(1, count) if k not in order]


def restored(items, order):
    order = arranged(order, len(items))
    return [items[0]] + [items[1 + order.index(k)] for k in range(1, len(items))]


def shifted(count, k):
    return [(i, (i + k) % count) for i in range(count)]


def ring_of(count):
    return RING if len(RING) == count else tuple(range(count))


def after(place, k, count):
    if XOR:
        return place ^ k
    ring = ring_of(count)
    if ring == tuple(range(count)):
        return lax.rem(place + k, count) if not isinstance(place, int) else (place + k) % count
    if isinstance(place, int):
        return ring[(ring.index(place) + k) % count]
    result = jnp.int32(0)
    for i in range(count):
        result = jnp.where(place == i, after(i, k, count), result)
    return result


def ringed(count, k):
    return [(i, after(i, k % count, count)) for i in range(count)]


def on_device(
    hidden,
    attention_norm_gain,
    row_adapter_index,
    lengths,
    paged_key_cache,
    paged_value_cache,
    query_weight,
    key_weight,
    value_weight,
    adapter_down_weight,
    adapter_up_query,
    adapter_up_key_value,
):
    wide, narrow = lax.axis_size("wide"), lax.axis_size("narrow")
    rows, features = hidden.shape
    count, _, rank, slice_width = adapter_down_weight.shape
    query_width, kv_width = query_weight.shape[1], key_weight.shape[1]
    heads, kv_heads = query_width // HEAD_WIDTH, kv_width // HEAD_WIDTH
    all_rows = rows * wide
    rank3 = 3 * rank
    width = query_width + 2 * kv_width
    half, wide_half = slice_width // 2, query_weight.shape[0] // 2

    message, *slices = call(
        functools.partial(normalize_kernel, wide),
        [shape_of((2 * rows, half + LANES), bf16)] + [shape_of((2 * rows, wide_half), bf16)] * wide,
        [HBM, HBM, HBM],
        [
            pltpu.with_memory_space_constraint(x, pltpu.HBM)
            for x in (row_adapter_index, hidden, attention_norm_gain)
        ],
        [
            pltpu.VMEM((rows, features), f32),
            pltpu.SMEM((rows,), jnp.int32),
            pltpu.VMEM((rows, features), bf16),
            pltpu.VMEM((features,), bf16),
            pltpu.SemaphoreType.DMA((3,)),
        ],
        flops=10**10,
    )
    blocks = [message] + [
        lax.ppermute(message, "wide", ringed(wide, k)) for k in arranged(N_ORDER, wide)
    ]
    wide_blocks = [slices[0]] + [
        lax.ppermute(slices[k], "wide", ringed(wide, k)) for k in arranged(W_ORDER, wide)
    ]
    down = adapter_down_weight.reshape(count * rank3, slice_width)
    sums, ids = call(
        functools.partial(down_kernel, wide, rank3),
        [shape_of((all_rows, rank3), f32), shape_of((all_rows, LANES), f32)],
        [VMEM] * wide + [VMEM],
        (*blocks, down),
        vmem=12,
        flops=2 * all_rows * down.size,
        nbytes=2 * down.size,
    )
    parts = [sums] + [lax.ppermute(sums, "narrow", shifted(narrow, k)) for k in range(1, narrow)]
    weights = (query_weight, key_weight, value_weight)
    base = call(
        functools.partial(base_kernel, wide),
        shape_of((all_rows, width), f32),
        [VMEM] * wide + [VMEM] * 3,
        (*wide_blocks, *weights),
        vmem=16,
        flops=4 * all_rows * width * wide_half,
        nbytes=4 * width * wide_half,
    )
    query_up = adapter_up_query.reshape(count * rank, query_width)
    body = width // LANES * rows
    step_rows = -(-rows // STEP_ROWS) * STEP_ROWS
    outs = call(
        functools.partial(up_kernel, wide, narrow),
        [shape_of((body, LANES), f32)]
        + [shape_of((body + step_rows, LANES), jnp.int16)] * (wide - 1),
        [VMEM, VMEM] + [VMEM] * narrow + [VMEM] * 2,
        (base, ids, *parts, query_up, adapter_up_key_value),
        [pltpu.VMEM((all_rows, width), f32), pltpu.VMEM((wide - 1, body, LANES), f32)],
        vmem=10 + wide // 2,
        flops=2 * all_rows * width * count * rank,
        nbytes=2 * width * count * rank,
    )
    gathered = [outs[0]] + [
        lax.ppermute(outs[k], "wide", ringed(wide, k if XOR else -k)) for k in arranged(O_ORDER, wide)
    ]
    turned = (heads + kv_heads) * rows
    cosine, sine, visible = call(
        rotation_kernel,
        [shape_of((turned, LANES), f32)] * 2 + [shape_of((rows, paged_key_cache.shape[2]), f32)],
        [HBM, ANY],
        (pltpu.with_memory_space_constraint(lengths, pltpu.HBM), outs[0]),
        [pltpu.SMEM((rows,), jnp.int32), pltpu.SemaphoreType.DMA],
    )
    return call(
        functools.partial(attend_kernel, wide, heads, kv_heads),
        shape_of((rows, query_width), bf16),
        [VMEM] * (3 + wide + 2),
        (visible, cosine, sine, *gathered, paged_key_cache, paged_value_cache),
        [
            pltpu.VMEM((body, LANES), f32),
            pltpu.VMEM((heads * rows, LANES), f32),
        ],
        vmem=8 + wide // 4,
        flops=4 * paged_key_cache.size * 8,
        nbytes=4 * paged_key_cache.size,
    )


def solution(mesh):
    in_specs = (
        P(("groups", "wide"), None),
        P(),
        P(("groups", "wide")),
        P(("groups", "wide")),
        P(("groups", "wide"), "narrow", None, None),
        P(("groups", "wide"), "narrow", None, None),
        P("wide", "narrow"),
        P("wide", "narrow"),
        P("wide", "narrow"),
        P(("groups", "wide"), None, None, "narrow"),
        P(("groups", "wide"), None, "narrow"),
        P(("groups", "wide"), None, None, "narrow"),
    )
    out_specs = P(("groups", "wide"), "narrow")
    return jax.shard_map(
        on_device, mesh=mesh, in_specs=in_specs, out_specs=out_specs, check_vma=False
    )
```

time: 121 us -> 32.5 us (0.27)
  blocking collectives: 34.5 us -> 0 us
  waiting for transfers between devices: 37.3 us -> 7.05 us
  matrix products: 16.4 us -> 0 us
  between operations: 15 us -> 0.12 us
  starting transfers between devices: 6.32 us -> 16.1 us
  Pallas kernels: 0 us -> 8.97 us
  other arithmetic: 6.35 us -> 0 us
  local copies, waits for them, and re-layouts: 4.98 us -> 0.05 us
    unnamed x2 -> x0, waiting for transfers between devices: 37.3 us -> none
    all_gather x1 -> x0, blocking collectives: 17.5 us -> none  [on_device(): lax.all_gather(my_slice, 'wide', axis=0, tiled=True)]
    dot_general x10 -> x0, matrix products: 16.4 us -> none  [the longest x3 5.68 us: on_device(): jnp.dot(feature_cols, matrix, preferred_element_type=jnp.float32)]
    ppermute x0 -> x12, starting transfers between devices: none -> 16.1 us  [the longest x3 6.11 us: on_device(): lax.ppermute(message, 'wide', ringed(wide, k))]
    psum x1 -> x0, blocking collectives: 10.5 us -> none  [on_device(): rank_sums = lax.psum(value_partial_sums, 'narrow').astype(jnp.bfloat16)]
    pallas_call x0 -> x6, Pallas kernels: none -> 8.97 us  [call(): pl.pallas_call(kernel, out_shape=outs, in_specs=in_specs, out_specs=jax.t...]
    ppermute x0 -> x12, waiting for transfers between devices: none -> 7.05 us  [the longest x3 4.04 us: on_device(): lax.ppermute(outs[k], 'wide', ringed(wide, k if XOR else -k))]
    unnamed x1 -> x0, blocking collectives: 6.5 us -> none
  transfers between devices with their start and end apart: 2 -> 12, of which waited for: 1 -> 6; matrix products, arithmetic and copies ran while one was open for 8% -> 0% of each run, Pallas kernels for 0% -> 15%
where the time goes in v1:
time: 32.5 us; the launch traced here: 32.3 us
  starting transfers between devices  16.1 us (50%)
  Pallas kernels  8.97 us (28%)
  waiting for transfers between devices  7.05 us (22%)
    pallas_call x6, Pallas kernels, call(): pl.pallas_call(kernel, out_shape=outs, in_specs=in_specs, out_specs=jax.t...  8.97 us
    ppermute x3, starting transfers between devices, on_device(): lax.ppermute(message, 'wide', ringed(wide, k))  6.11 us
    ppermute x3, starting transfers between devices, on_device(): lax.ppermute(slices[k], 'wide', ringed(wide, k))  5.54 us
    ppermute x3, waiting for transfers between devices, on_device(): lax.ppermute(outs[k], 'wide', ringed(wide, k if XOR else -k))  4.04 us
    ppermute x3, starting transfers between devices, on_device(): lax.ppermute(outs[k], 'wide', ringed(wide, k if XOR else -k))  2.71 us
    ppermute x3, starting transfers between devices, on_device(): lax.ppermute(sums, 'narrow', shifted(narrow, k))  1.78 us
    ppermute x3, waiting for transfers between devices, on_device(): lax.ppermute(message, 'wide', ringed(wide, k))  1.59 us
    ppermute x3, waiting for transfers between devices, on_device(): lax.ppermute(sums, 'narrow', shifted(narrow, k))  1.41 us
  transfers between devices with their start and end apart: 12, of which 6 were waited for; matrix products, arithmetic and copies ran while one was open for 0% of the time, Pallas kernels for 15%

profile of v1, /device:TPU:0, one launch (start us, length us, event | category | flops | bytes accessed | tf_op | source)
XLA Modules:
  0.0 32.3 jit_solution(7264270926580880873)
XLA Ops:
  0.0 1.5 %shard_map.118 = (bf16[24,1152]{1,0:T(8,128)(2,1)S(1)}, bf16[24,1024]{1,0:T(8,128)(2,1)S(1)}, bf16[24,1024]{1,0:T(8,128)(2,1)S(1)}, bf16[24,1024]{1,0:T(8,128)(2,1)S(1)}, bf16[24,1024]{1,0:T(8,128)(2,1)S(1)}) custom-call(s32[12]{0:T(128)} %index_far.1, bf16[12,8192]{1,0:T(8,128)(2,1)} %hidden_far.1, bf16[8192]{0:T(1024)(128)(2,1)} %gain_far.1), custom_call_target="tpu_custom_call" | custom-call | flops 10000000000 | tf_op jit(solution)/shard_map/pallas_call | solution.py:37
  1.5 5.1 %collective-permute-start.5 = (bf16[24,1152]{1,0:T(8,128)(2,1)S(1)}, bf16[24,1152]{1,0:T(8,128)(2,1)S(1)}, u32[]{:S(2)}, u32[]{:S(2)}) collective-permute-start(bf16[24,1152]{1,0:T(8,128)(2,1)S(1)} %get-tuple-element.23.refs_0_), channel_id=1, source_target_pairs={{0,12},{4,0},{8,4},{12,8},{1,13},{5,1},{9,5},{13,9},{2,14},{6,2},{... | collective-permute-start | bytes 165896 | tf_op jit(solution)/shard_map/ppermute | solution.py:366
  6.6 0.0 collective-permute-start.4
  6.6 1.0 %collective-permute-start.3 = (bf16[24,1152]{1,0:T(8,128)(2,1)S(1)}, bf16[24,1152]{1,0:T(8,128)(2,1)S(1)}, u32[]{:S(2)}, u32[]{:S(2)}) collective-permute-start(bf16[24,1152]{1,0:T(8,128)(2,1)S(1)} %get-tuple-element.23.refs_0_), channel_id=1, source_target_pairs={{0,4},{4,8},{8,12},{12,0},{1,5},{5,9},{9,13},{13,1},{2,6},{6,10},{... | collective-permute-start | bytes 165896 | tf_op jit(solution)/shard_map/ppermute | solution.py:366
  7.6 2.5 %collective-permute-start = (bf16[24,1024]{1,0:T(8,128)(2,1)S(1)}, bf16[24,1024]{1,0:T(8,128)(2,1)S(1)}, u32[]{:S(2)}, u32[]{:S(2)}) collective-permute-start(bf16[24,1024]{1,0:T(8,128)(2,1)S(1)} %get-tuple-element.20), channel_id=1, source_target_pairs={{0,4},{4,8},{8,12},{12,0},{1,5},{5,9},{9,13},{13,1},{2,6},{6,10},{... | collective-permute-start | bytes 147464 | tf_op jit(solution)/shard_map/ppermute | solution.py:369
  10.1 0.9 %collective-permute-start.1 = (bf16[24,1024]{1,0:T(8,128)(2,1)S(1)}, bf16[24,1024]{1,0:T(8,128)(2,1)S(1)}, u32[]{:S(2)}, u32[]{:S(2)}) collective-permute-start(bf16[24,1024]{1,0:T(8,128)(2,1)S(1)} %get-tuple-element.21), channel_id=1, source_target_pairs={{0,8},{4,12},{8,0},{12,4},{1,9},{5,13},{9,1},{13,5},{2,10},{6,14},... | collective-permute-start | bytes 147464 | tf_op jit(solution)/shard_map/ppermute | solution.py:369
  11.0 2.2 %collective-permute-start.2 = (bf16[24,1024]{1,0:T(8,128)(2,1)S(1)}, bf16[24,1024]{1,0:T(8,128)(2,1)S(1)}, u32[]{:S(2)}, u32[]{:S(2)}) collective-permute-start(bf16[24,1024]{1,0:T(8,128)(2,1)S(1)} %get-tuple-element.22), channel_id=1, source_target_pairs={{0,12},{4,0},{8,4},{12,8},{1,13},{5,1},{9,5},{13,9},{2,14},{6,2},{... | collective-permute-start | bytes 147464 | tf_op jit(solution)/shard_map/ppermute | solution.py:369
  13.2 1.6 %collective-permute-done.4.refs_2_ = bf16[24,1152]{1,0:T(8,128)(2,1)S(1)} collective-permute-done((bf16[24,1152]{1,0:T(8,128)(2,1)S(1)}, bf16[24,1152]{1,0:T(8,128)(2,1)S(1)}, u32[]{:S(2)}, u32[]{:S(2)}) %collective-permute-start.4) | collective-permute-done | bytes 55328 | tf_op jit(solution)/shard_map/ppermute | solution.py:366
  14.8 0.0 copy-start.6
  14.8 2.1 %shard_map.120 = (f32[48,192]{1,0:T(8,128)S(1)}, f32[48,128]{1,0:T(8,128)S(1)}) custom-call(bf16[24,1152]{1,0:T(8,128)(2,1)S(1)} %get-tuple-element.23.refs_0_, bf16[24,1152]{1,0:T(8,128)(2,1)S(1)} %collective-permute-done.3.refs_1_, bf16[24,1152]{1,0:T(8,128)(2,1)S(1)} %collective-permute-done.4.refs_2_, ...), custom_call_target="tpu_custom_call" | custom-call | flops 301989888 | bytes 6291456 | tf_op jit(solution)/shard_map/pallas_call | solution.py:37
  16.9 0.1 collective-permute-start.8
  16.9 1.6 %collective-permute-start.7 = (f32[48,192]{1,0:T(8,128)S(1)}, f32[48,192]{1,0:T(8,128)S(1)}, u32[]{:S(2)}, u32[]{:S(2)}) collective-permute-start(f32[48,192]{1,0:T(8,128)S(1)} %get-tuple-element.25.refs_0_), channel_id=1, source_target_pairs={{0,2},{1,3},{2,0},{3,1},{4,6},{5,7},{6,4},{7,5},{8,10},{9,11},{10,... | collective-permute-start | bytes 110600 | tf_op jit(solution)/shard_map/ppermute | solution.py:381
  18.5 0.0 collective-permute-done.refs_1_
  18.5 0.2 collective-permute-start.6
  18.7 0.0 collective-permute-done.1.refs_2_
  18.7 0.0 collective-permute-done.2.refs_3_
  18.7 0.0 copy-start.2
  18.7 0.0 copy-start.7
  18.7 1.9 %shard_map.119.base = f32[48,2560]{1,0:T(8,128)S(1)} custom-call(bf16[24,1024]{1,0:T(8,128)(2,1)S(1)} %get-tuple-element.19.refs_0_, bf16[24,1024]{1,0:T(8,128)(2,1)S(1)} %collective-permute-done.refs_1_, bf16[24,1024]{1,0:T(8,128)(2,1)S(1)} %collective-permute-done.1.refs_2_, bf16[24,1024]{1,0:T(8,128)(2,1)S(1)} %collective-permute-done.2.refs_3_, ...), custom_call_target="tpu_custom_call" | custom-call | flops 503316480 | bytes 10485760 | tf_op jit(solution)/shard_map/pallas_call | solution.py:37
  20.6 0.0 copy-start.3
  20.6 0.0 copy-start.4
  20.7 0.9 %collective-permute-done.7.refs_2_ = f32[48,192]{1,0:T(8,128)S(1)} collective-permute-done((f32[48,192]{1,0:T(8,128)S(1)}, f32[48,192]{1,0:T(8,128)S(1)}, u32[]{:S(2)}, u32[]{:S(2)}) %collective-permute-start.7) | collective-permute-done | bytes 36896 | tf_op jit(solution)/shard_map/ppermute | solution.py:381
  21.5 0.5 %collective-permute-done.6.refs_1_ = f32[48,192]{1,0:T(8,128)S(1)} collective-permute-done((f32[48,192]{1,0:T(8,128)S(1)}, f32[48,192]{1,0:T(8,128)S(1)}, u32[]{:S(2)}, u32[]{:S(2)}) %collective-permute-start.6) | collective-permute-done | bytes 36896 | tf_op jit(solution)/shard_map/ppermute | solution.py:381
  22.1 0.8 %shard_map.121 = (f32[240,128]{1,0:T(8,128)S(1)}, s16[256,128]{1,0:T(8,128)(2,1)S(1)}, s16[256,128]{1,0:T(8,128)(2,1)S(1)}, s16[256,128]{1,0:T(8,128)(2,1)S(1)}) custom-call(f32[48,2560]{1,0:T(8,128)S(1)} %shard_map.119.base, f32[48,128]{1,0:T(8,128)S(1)} %get-tuple-element.24.ids, f32[48,192]{1,0:T(8,128)S(1)} %get-tuple-element.25.refs_0_, ...), custom_call_target="tpu_custom_call" | custom-call | flops 125829120 | bytes 2621440 | tf_op jit(solution)/shard_map/pallas_call | solution.py:37
  22.9 0.7 %collective-permute-start.9 = (s16[256,128]{1,0:T(8,128)(2,1)S(1)}, s16[256,128]{1,0:T(8,128)(2,1)S(1)}, u32[]{:S(2)}, u32[]{:S(2)}) collective-permute-start(s16[256,128]{1,0:T(8,128)(2,1)S(1)} %get-tuple-element.30), channel_id=1, source_target_pairs={{0,8},{4,12},{8,0},{12,4},{1,9},{5,13},{9,1},{13,5},{2,10},{6,14},... | collective-permute-start | bytes 196616 | tf_op jit(solution)/shard_map/ppermute | solution.py:407
  23.6 0.4 %collective-permute-start.10 = (s16[256,128]{1,0:T(8,128)(2,1)S(1)}, s16[256,128]{1,0:T(8,128)(2,1)S(1)}, u32[]{:S(2)}, u32[]{:S(2)}) collective-permute-start(s16[256,128]{1,0:T(8,128)(2,1)S(1)} %get-tuple-element.31), channel_id=1, source_target_pairs={{0,12},{4,0},{8,4},{12,8},{1,13},{5,1},{9,5},{13,9},{2,14},{6,2},{... | collective-permute-start | bytes 196616 | tf_op jit(solution)/shard_map/ppermute | solution.py:407
  24.0 1.6 %collective-permute-start.11 = (s16[256,128]{1,0:T(8,128)(2,1)S(1)}, s16[256,128]{1,0:T(8,128)(2,1)S(1)}, u32[]{:S(2)}, u32[]{:S(2)}) collective-permute-start(s16[256,128]{1,0:T(8,128)(2,1)S(1)} %get-tuple-element.32), channel_id=1, source_target_pairs={{0,4},{4,8},{8,12},{12,0},{1,5},{5,9},{9,13},{13,1},{2,6},{6,10},{... | collective-permute-start | bytes 196616 | tf_op jit(solution)/shard_map/ppermute | solution.py:407
  25.6 0.7 %shard_map.122 = (f32[216,128]{1,0:T(8,128)S(1)}, f32[216,128]{1,0:T(8,128)S(1)}, f32[12,192]{1,0:T(8,128)S(1)}) custom-call(s32[12]{0:T(128)} %lengths_far.1, f32[240,128]{1,0:T(8,128)S(1)} %get-tuple-element.26.after.refs_0_), custom_call_target="tpu_custom_call" | custom-call | tf_op jit(solution)/shard_map/pallas_call | solution.py:37
  26.3 2.7 %collective-permute-done.9.refs_1_ = s16[256,128]{1,0:T(8,128)(2,1)S(1)} collective-permute-done((s16[256,128]{1,0:T(8,128)(2,1)S(1)}, s16[256,128]{1,0:T(8,128)(2,1)S(1)}, u32[]{:S(2)}, u32[]{:S(2)}) %collective-permute-start.9) | collective-permute-done | bytes 65568 | tf_op jit(solution)/shard_map/ppermute | solution.py:407
  29.1 0.2 collective-permute-done.10.refs_2_
  29.2 1.1 %collective-permute-done.11.refs_3_ = s16[256,128]{1,0:T(8,128)(2,1)S(1)} collective-permute-done((s16[256,128]{1,0:T(8,128)(2,1)S(1)}, s16[256,128]{1,0:T(8,128)(2,1)S(1)}, u32[]{:S(2)}, u32[]{:S(2)}) %collective-permute-start.11) | collective-permute-done | bytes 65568 | tf_op jit(solution)/shard_map/ppermute | solution.py:407
  30.4 1.9 %shard_map.123 = bf16[12,2048]{1,0:T(8,128)(2,1)} custom-call(f32[12,192]{1,0:T(8,128)S(1)} %get-tuple-element.27.visible, f32[216,128]{1,0:T(8,128)S(1)} %get-tuple-element.28.cosine, f32[216,128]{1,0:T(8,128)S(1)} %get-tuple-element.29.sine, f32[240,128]{1,0:T(8,128)S(1)} %get-tuple-element.26.after.refs_0_, ...), custom_call_target="tpu_custom_call" | custom-call | flops 18874368 | bytes 2359296 | tf_op jit(solution)/shard_map/pallas_call | solution.py:37
  (14 shorter events, 0.0 us)
Async XLA Ops:
  0.0 14.8 %copy-start.1 = (bf16[8,3,64,2048]{3,2,1,0:T(8,128)(2,1)S(1)}, bf16[8,3,64,2048]{3,2,1,0:T(8,128)(2,1)}, u32[]{:S(2)}) copy-start(bf16[8,3,64,2048]{3,2,1,0:T(8,128)(2,1)} %param.21) | copy-start | bytes 18874372
  0.0 18.7 %copy-start = (bf16[2048,2048]{1,0:T(8,128)(2,1)S(1)}, bf16[2048,2048]{1,0:T(8,128)(2,1)}, u32[]{:S(2)}) copy-start(bf16[2048,2048]{1,0:T(8,128)(2,1)} %refs_4_.2) | copy-start | bytes 25165828
  1.5 9.5 %collective-permute-start.5 = (bf16[24,1152]{1,0:T(8,128)(2,1)S(1)}, bf16[24,1152]{1,0:T(8,128)(2,1)S(1)}, u32[]{:S(2)}, u32[]{:S(2)}) collective-permute-start(bf16[24,1152]{1,0:T(8,128)(2,1)S(1)} %get-tuple-element.23.refs_0_), channel_id=1, source_target_pairs={{0,12},{4,0},{8,4},{12,8},{1,13},{5,1},{9,5},{13,9},{2,14},{6,2},{... | collective-permute-start | bytes 165896 | tf_op jit(solution)/shard_map/ppermute | solution.py:366
  6.6 8.1 %collective-permute-start.4 = (bf16[24,1152]{1,0:T(8,128)(2,1)S(1)}, bf16[24,1152]{1,0:T(8,128)(2,1)S(1)}, u32[]{:S(2)}, u32[]{:S(2)}) collective-permute-start(bf16[24,1152]{1,0:T(8,128)(2,1)S(1)} %get-tuple-element.23.refs_0_), channel_id=1, source_target_pairs={{0,8},{4,12},{8,0},{12,4},{1,9},{5,13},{9,1},{13,5},{2,10},{6,14},... | collective-permute-start | bytes 165896 | tf_op jit(solution)/shard_map/ppermute | solution.py:366
  6.6 8.1 %collective-permute-start.3 = (bf16[24,1152]{1,0:T(8,128)(2,1)S(1)}, bf16[24,1152]{1,0:T(8,128)(2,1)S(1)}, u32[]{:S(2)}, u32[]{:S(2)}) collective-permute-start(bf16[24,1152]{1,0:T(8,128)(2,1)S(1)} %get-tuple-element.23.refs_0_), channel_id=1, source_target_pairs={{0,4},{4,8},{8,12},{12,0},{1,5},{5,9},{9,13},{13,1},{2,6},{6,10},{... | collective-permute-start | bytes 165896 | tf_op jit(solution)/shard_map/ppermute | solution.py:366
  7.6 10.9 %collective-permute-start = (bf16[24,1024]{1,0:T(8,128)(2,1)S(1)}, bf16[24,1024]{1,0:T(8,128)(2,1)S(1)}, u32[]{:S(2)}, u32[]{:S(2)}) collective-permute-start(bf16[24,1024]{1,0:T(8,128)(2,1)S(1)} %get-tuple-element.20), channel_id=1, source_target_pairs={{0,4},{4,8},{8,12},{12,0},{1,5},{5,9},{9,13},{13,1},{2,6},{6,10},{... | collective-permute-start | bytes 147464 | tf_op jit(solution)/shard_map/ppermute | solution.py:369
  10.1 8.6 %collective-permute-start.1 = (bf16[24,1024]{1,0:T(8,128)(2,1)S(1)}, bf16[24,1024]{1,0:T(8,128)(2,1)S(1)}, u32[]{:S(2)}, u32[]{:S(2)}) collective-permute-start(bf16[24,1024]{1,0:T(8,128)(2,1)S(1)} %get-tuple-element.21), channel_id=1, source_target_pairs={{0,8},{4,12},{8,0},{12,4},{1,9},{5,13},{9,1},{13,5},{2,10},{6,14},... | collective-permute-start | bytes 147464 | tf_op jit(solution)/shard_map/ppermute | solution.py:369
  11.0 7.7 %collective-permute-start.2 = (bf16[24,1024]{1,0:T(8,128)(2,1)S(1)}, bf16[24,1024]{1,0:T(8,128)(2,1)S(1)}, u32[]{:S(2)}, u32[]{:S(2)}) collective-permute-start(bf16[24,1024]{1,0:T(8,128)(2,1)S(1)} %get-tuple-element.22), channel_id=1, source_target_pairs={{0,12},{4,0},{8,4},{12,8},{1,13},{5,1},{9,5},{13,9},{2,14},{6,2},{... | collective-permute-start | bytes 147464 | tf_op jit(solution)/shard_map/ppermute | solution.py:369
  14.8 3.9 %copy-start.5 = (bf16[2048,256]{1,0:T(8,128)(2,1)S(1)}, bf16[2048,256]{1,0:T(8,128)(2,1)}, u32[]{:S(2)}) copy-start(bf16[2048,256]{1,0:T(8,128)(2,1)} %refs_5_.3) | copy-start | bytes 3145732
  14.8 3.9 %copy-start.6 = (bf16[2048,256]{1,0:T(8,128)(2,1)S(1)}, bf16[2048,256]{1,0:T(8,128)(2,1)}, u32[]{:S(2)}) copy-start(bf16[2048,256]{1,0:T(8,128)(2,1)} %refs_6_.1) | copy-start | bytes 3145732
  16.9 3.8 %collective-permute-start.8 = (f32[48,192]{1,0:T(8,128)S(1)}, f32[48,192]{1,0:T(8,128)S(1)}, u32[]{:S(2)}, u32[]{:S(2)}) collective-permute-start(f32[48,192]{1,0:T(8,128)S(1)} %get-tuple-element.25.refs_0_), channel_id=1, source_target_pairs={{0,3},{1,0},{2,1},{3,2},{4,7},{5,4},{6,5},{7,6},{8,11},{9,8},{10,9... | collective-permute-start | bytes 110600 | tf_op jit(solution)/shard_map/ppermute | solution.py:381
  16.9 4.6 %collective-permute-start.7 = (f32[48,192]{1,0:T(8,128)S(1)}, f32[48,192]{1,0:T(8,128)S(1)}, u32[]{:S(2)}, u32[]{:S(2)}) collective-permute-start(f32[48,192]{1,0:T(8,128)S(1)} %get-tuple-element.25.refs_0_), channel_id=1, source_target_pairs={{0,2},{1,3},{2,0},{3,1},{4,6},{5,7},{6,4},{7,5},{8,10},{9,11},{10,... | collective-permute-start | bytes 110600 | tf_op jit(solution)/shard_map/ppermute | solution.py:381
  18.5 3.6 %collective-permute-start.6 = (f32[48,192]{1,0:T(8,128)S(1)}, f32[48,192]{1,0:T(8,128)S(1)}, u32[]{:S(2)}, u32[]{:S(2)}) collective-permute-start(f32[48,192]{1,0:T(8,128)S(1)} %get-tuple-element.25.refs_0_), channel_id=1, source_target_pairs={{0,1},{1,2},{2,3},{3,0},{4,5},{5,6},{6,7},{7,4},{8,9},{9,10},{10,1... | collective-permute-start | bytes 110600 | tf_op jit(solution)/shard_map/ppermute | solution.py:381
  18.7 3.4 %copy-start.2 = (bf16[8,64,2048]{2,1,0:T(8,128)(2,1)S(1)}, bf16[8,64,2048]{2,1,0:T(8,128)(2,1)}, u32[]{:S(2)}) copy-start(bf16[8,64,2048]{2,1,0:T(8,128)(2,1)} %param.22) | copy-start | bytes 6291460
  18.7 3.4 %copy-start.7 = (bf16[8,2,64,256]{3,2,1,0:T(8,128)(2,1)S(1)}, bf16[8,2,64,256]{3,2,1,0:T(8,128)(2,1)}, u32[]{:S(2)}) copy-start(bf16[8,2,64,256]{3,2,1,0:T(8,128)(2,1)} %refs_5_.4) | copy-start | bytes 1572868
  20.6 9.8 %copy-start.3 = (bf16[12,2,192,128]{3,2,1,0:T(8,128)(2,1)S(1)}, bf16[12,2,192,128]{3,2,1,0:T(8,128)(2,1)}, u32[]{:S(2)}) copy-start(bf16[12,2,192,128]{3,2,1,0:T(8,128)(2,1)} %refs_4_.3) | copy-start | bytes 3538948
  20.6 9.8 %copy-start.4 = (bf16[12,2,192,128]{3,2,1,0:T(8,128)(2,1)S(1)}, bf16[12,2,192,128]{3,2,1,0:T(8,128)(2,1)}, u32[]{:S(2)}) copy-start(bf16[12,2,192,128]{3,2,1,0:T(8,128)(2,1)} %refs_5_.5) | copy-start | bytes 3538948
  22.9 6.2 %collective-permute-start.9 = (s16[256,128]{1,0:T(8,128)(2,1)S(1)}, s16[256,128]{1,0:T(8,128)(2,1)S(1)}, u32[]{:S(2)}, u32[]{:S(2)}) collective-permute-start(s16[256,128]{1,0:T(8,128)(2,1)S(1)} %get-tuple-element.30), channel_id=1, source_target_pairs={{0,8},{4,12},{8,0},{12,4},{1,9},{5,13},{9,1},{13,5},{2,10},{6,14},... | collective-permute-start | bytes 196616 | tf_op jit(solution)/shard_map/ppermute | solution.py:407
  23.6 5.7 %collective-permute-start.10 = (s16[256,128]{1,0:T(8,128)(2,1)S(1)}, s16[256,128]{1,0:T(8,128)(2,1)S(1)}, u32[]{:S(2)}, u32[]{:S(2)}) collective-permute-start(s16[256,128]{1,0:T(8,128)(2,1)S(1)} %get-tuple-element.31), channel_id=1, source_target_pairs={{0,12},{4,0},{8,4},{12,8},{1,13},{5,1},{9,5},{13,9},{2,14},{6,2},{... | collective-permute-start | bytes 196616 | tf_op jit(solution)/shard_map/ppermute | solution.py:407
  24.0 6.4 %collective-permute-start.11 = (s16[256,128]{1,0:T(8,128)(2,1)S(1)}, s16[256,128]{1,0:T(8,128)(2,1)S(1)}, u32[]{:S(2)}, u32[]{:S(2)}) collective-permute-start(s16[256,128]{1,0:T(8,128)(2,1)S(1)} %get-tuple-element.32), channel_id=1, source_target_pairs={{0,4},{4,8},{8,12},{12,0},{1,5},{5,9},{9,13},{13,1},{2,6},{6,10},{... | collective-permute-start | bytes 196616 | tf_op jit(solution)/shard_map/ppermute | solution.py:407

commit v2 on v1

--- a/solution.py
+++ b/solution.py
@@ -15,11 +15,7 @@
 rope_base = 500000.0
 epsilon = 1e-05
 
-RING = (0, 1, 2, 3)
-XOR = False
-N_ORDER = (1, 2, 3)
-W_ORDER = (1, 2, 3)
-O_ORDER = (2, 1, 3)
+LAST_ORDER = (2, 3, 1)
 
 f32 = jnp.float32
 bf16 = jnp.bfloat16
@@ -88,7 +84,7 @@
         ids = jnp.where((row == r) | (row == r + rows), index[r].astype(f32), ids)
     message[:, half:] = ids.astype(bf16)
     for k in range(wide):
-        target = after(wide_place, k, wide)
+        target = lax.bitwise_xor(wide_place, k)
         slices[k][...] = stacked(target * (2 * wide_half), wide_half)
 
 
@@ -104,7 +100,7 @@
     blocks, down, (sums, ids) = refs[:wide], refs[wide], refs[wide + 1 :]
     wide_place, _ = own_place()
     count = down.shape[0] // rank3
-    upper, lower = joined(restored(blocks, N_ORDER))
+    upper, lower = joined(blocks)
     half = upper.shape[1] - LANES
     row_ids = upper[:, half:]
     ids[...] = row_ids
@@ -125,7 +121,7 @@
 def base_kernel(wide, *refs):
     blocks, sources, out = refs[:wide], refs[wide:-1], refs[-1]
     chunk = 256
-    upper, lower = (part.astype(bf16) for part in joined(restored(blocks, W_ORDER)))
+    upper, lower = (part.astype(bf16) for part in joined(blocks))
     half = upper.shape[1]
     offset = 0
     for source in sources:
@@ -286,39 +282,12 @@
     sine[...] = jnp.concatenate([sines] * repeats, axis=0)
 
 
-def arranged(order, count):
-    return [k for k in order if k < count] + [k for k in range(1, count) if k not in order]
-
-
-def restored(items, order):
-    order = arranged(order, len(items))
-    return [items[0]] + [items[1 + order.index(k)] for k in range(1, len(items))]
-
-
 def shifted(count, k):
     return [(i, (i + k) % count) for i in range(count)]
 
 
-def ring_of(count):
-    return RING if len(RING) == count else tuple(range(count))
-
-
-def after(place, k, count):
-    if XOR:
-        return place ^ k
-    ring = ring_of(count)
-    if ring == tuple(range(count)):
-        return lax.rem(place + k, count) if not isinstance(place, int) else (place + k) % count
-    if isinstance(place, int):
-        return ring[(ring.index(place) + k) % count]
-    result = jnp.int32(0)
-    for i in range(count):
-        result = jnp.where(place == i, after(i, k, count), result)
-    return result
-
-
-def ringed(count, k):
-    return [(i, after(i, k % count, count)) for i in range(count)]
+def paired(count, k):
+    return [(i, i ^ k) for i in range(count)]
 
 
 def on_device(
@@ -363,10 +332,10 @@
         flops=10**10,
     )
     blocks = [message] + [
-        lax.ppermute(message, "wide", ringed(wide, k)) for k in arranged(N_ORDER, wide)
+        lax.ppermute(message, "wide", paired(wide, k)) for k in range(1, wide)
     ]
     wide_blocks = [slices[0]] + [
-        lax.ppermute(slices[k], "wide", ringed(wide, k)) for k in arranged(W_ORDER, wide)
+        lax.ppermute(slices[k], "wide", paired(wide, k)) for k in range(1, wide)
     ]
     down = adapter_down_weight.reshape(count * rank3, slice_width)
     sums, ids = call(
@@ -404,7 +373,8 @@
         nbytes=2 * width * count * rank,
     )
     gathered = [outs[0]] + [
-        lax.ppermute(outs[k], "wide", ringed(wide, k if XOR else -k)) for k in arranged(O_ORDER, wide)
+        lax.ppermute(outs[k], "wide", paired(wide, k))
+        for k in (LAST_ORDER if wide == 4 else range(1, wide))
     ]
     turned = (heads + kv_heads) * rows
     cosine, sine, visible = call(

time: 32.5 us -> 31.2 us (0.960)
  waiting for transfers between devices: 7.05 us -> 4.84 us
  starting transfers between devices: 16.1 us -> 17.1 us
    ppermute x9, waiting for transfers between devices: 5.64 us -> 3.72 us  [the longest x3 3.4 us: on_device(): lax.ppermute(outs[k], 'wide', paired(wide, k))]
    ppermute x9, starting transfers between devices: 14.4 us -> 15.3 us  [the longest x3 5.97 us: on_device(): lax.ppermute(slices[k], 'wide', paired(wide, k))]
  transfers between devices with their start and end apart: 12 -> 12, of which waited for: 6 -> 5; matrix products, arithmetic and copies ran while one was open for 0% -> 0% of each run, Pallas kernels for 15% -> 15%
where the time goes in v2:
time: 31.2 us; the launch traced here: 31 us
  starting transfers between devices  17.1 us (55%)
  Pallas kernels  8.97 us (29%)
  waiting for transfers between devices  4.84 us (16%)
    pallas_call x6, Pallas kernels, call(): pl.pallas_call(kernel, out_shape=outs, in_specs=in_specs, out_specs=jax.t...  8.97 us
    ppermute x3, starting transfers between devices, on_device(): lax.ppermute(slices[k], 'wide', paired(wide, k))  5.97 us
    ppermute x3, starting transfers between devices, on_device(): lax.ppermute(message, 'wide', paired(wide, k))  5.76 us
    ppermute x3, starting transfers between devices, on_device(): lax.ppermute(outs[k], 'wide', paired(wide, k))  3.55 us
    ppermute x3, waiting for transfers between devices, on_device(): lax.ppermute(outs[k], 'wide', paired(wide, k))  3.4 us
    ppermute x3, starting transfers between devices, on_device(): lax.ppermute(sums, 'narrow', shifted(narrow, k))  1.78 us
    ppermute x3, waiting for transfers between devices, on_device(): lax.ppermute(sums, 'narrow', shifted(narrow, k))  1.12 us
  transfers between devices with their start and end apart: 12, of which 5 were waited for; matrix products, arithmetic and copies ran while one was open for 0% of the time, Pallas kernels for 15%

profile of v2, /device:TPU:0, one launch (start us, length us, event | category | flops | bytes accessed | tf_op | source)
XLA Modules:
  0.0 31.0 jit_solution(11131402633393627710)
XLA Ops:
  0.0 1.5 %shard_map.118 = (bf16[24,1152]{1,0:T(8,128)(2,1)S(1)}, bf16[24,1024]{1,0:T(8,128)(2,1)S(1)}, bf16[24,1024]{1,0:T(8,128)(2,1)S(1)}, bf16[24,1024]{1,0:T(8,128)(2,1)S(1)}, bf16[24,1024]{1,0:T(8,128)(2,1)S(1)}) custom-call(s32[12]{0:T(128)} %index_far.1, bf16[12,8192]{1,0:T(8,128)(2,1)} %hidden_far.1, bf16[8192]{0:T(1024)(128)(2,1)} %gain_far.1), custom_call_target="tpu_custom_call" | custom-call | flops 10000000000 | tf_op jit(solution)/shard_map/pallas_call | solution.py:33
  1.5 5.1 %collective-permute-start.5 = (bf16[24,1152]{1,0:T(8,128)(2,1)S(1)}, bf16[24,1152]{1,0:T(8,128)(2,1)S(1)}, u32[]{:S(2)}, u32[]{:S(2)}) collective-permute-start(bf16[24,1152]{1,0:T(8,128)(2,1)S(1)} %get-tuple-element.23.refs_0_), channel_id=1, source_target_pairs={{0,12},{4,8},{8,4},{12,0},{1,13},{5,9},{9,5},{13,1},{2,14},{6,10},... | collective-permute-start | bytes 165896 | tf_op jit(solution)/shard_map/ppermute | solution.py:335
  6.6 0.0 collective-permute-start.4
  6.6 0.6 %collective-permute-start.3 = (bf16[24,1152]{1,0:T(8,128)(2,1)S(1)}, bf16[24,1152]{1,0:T(8,128)(2,1)S(1)}, u32[]{:S(2)}, u32[]{:S(2)}) collective-permute-start(bf16[24,1152]{1,0:T(8,128)(2,1)S(1)} %get-tuple-element.23.refs_0_), channel_id=1, source_target_pairs={{0,4},{4,0},{8,12},{12,8},{1,5},{5,1},{9,13},{13,9},{2,6},{6,2},{1... | collective-permute-start | bytes 165896 | tf_op jit(solution)/shard_map/ppermute | solution.py:335
  7.3 1.4 %collective-permute-start = (bf16[24,1024]{1,0:T(8,128)(2,1)S(1)}, bf16[24,1024]{1,0:T(8,128)(2,1)S(1)}, u32[]{:S(2)}, u32[]{:S(2)}) collective-permute-start(bf16[24,1024]{1,0:T(8,128)(2,1)S(1)} %get-tuple-element.20), channel_id=1, source_target_pairs={{0,4},{4,0},{8,12},{12,8},{1,5},{5,1},{9,13},{13,9},{2,6},{6,2},{1... | collective-permute-start | bytes 147464 | tf_op jit(solution)/shard_map/ppermute | solution.py:338
  8.7 2.9 %collective-permute-start.1 = (bf16[24,1024]{1,0:T(8,128)(2,1)S(1)}, bf16[24,1024]{1,0:T(8,128)(2,1)S(1)}, u32[]{:S(2)}, u32[]{:S(2)}) collective-permute-start(bf16[24,1024]{1,0:T(8,128)(2,1)S(1)} %get-tuple-element.21), channel_id=1, source_target_pairs={{0,8},{4,12},{8,0},{12,4},{1,9},{5,13},{9,1},{13,5},{2,10},{6,14},... | collective-permute-start | bytes 147464 | tf_op jit(solution)/shard_map/ppermute | solution.py:338
  11.6 0.0 collective-permute-done.5.refs_3_
  11.6 1.7 %collective-permute-start.2 = (bf16[24,1024]{1,0:T(8,128)(2,1)S(1)}, bf16[24,1024]{1,0:T(8,128)(2,1)S(1)}, u32[]{:S(2)}, u32[]{:S(2)}) collective-permute-start(bf16[24,1024]{1,0:T(8,128)(2,1)S(1)} %get-tuple-element.22), channel_id=1, source_target_pairs={{0,12},{4,8},{8,4},{12,0},{1,13},{5,9},{9,5},{13,1},{2,14},{6,10},... | collective-permute-start | bytes 147464 | tf_op jit(solution)/shard_map/ppermute | solution.py:338
  13.2 0.0 collective-permute-done.4.refs_2_
  13.2 0.0 copy-start.5
  13.3 0.0 copy-start.6
  13.3 2.1 %shard_map.120 = (f32[48,192]{1,0:T(8,128)S(1)}, f32[48,128]{1,0:T(8,128)S(1)}) custom-call(bf16[24,1152]{1,0:T(8,128)(2,1)S(1)} %get-tuple-element.23.refs_0_, bf16[24,1152]{1,0:T(8,128)(2,1)S(1)} %collective-permute-done.3.refs_1_, bf16[24,1152]{1,0:T(8,128)(2,1)S(1)} %collective-permute-done.4.refs_2_, ...), custom_call_target="tpu_custom_call" | custom-call | flops 301989888 | bytes 6291456 | tf_op jit(solution)/shard_map/pallas_call | solution.py:33
  15.4 0.1 collective-permute-start.8
  15.4 1.6 %collective-permute-start.7 = (f32[48,192]{1,0:T(8,128)S(1)}, f32[48,192]{1,0:T(8,128)S(1)}, u32[]{:S(2)}, u32[]{:S(2)}) collective-permute-start(f32[48,192]{1,0:T(8,128)S(1)} %get-tuple-element.25.refs_0_), channel_id=1, source_target_pairs={{0,2},{1,3},{2,0},{3,1},{4,6},{5,7},{6,4},{7,5},{8,10},{9,11},{10,... | collective-permute-start | bytes 110600 | tf_op jit(solution)/shard_map/ppermute | solution.py:350
  17.0 0.2 collective-permute-start.6
  17.2 0.3 collective-permute-done.2.refs_3_
  17.5 0.0 copy-start.2
  17.5 0.0 copy-start.7
  17.5 1.9 %shard_map.119.base = f32[48,2560]{1,0:T(8,128)S(1)} custom-call(bf16[24,1024]{1,0:T(8,128)(2,1)S(1)} %get-tuple-element.19.refs_0_, bf16[24,1024]{1,0:T(8,128)(2,1)S(1)} %collective-permute-done.refs_1_, bf16[24,1024]{1,0:T(8,128)(2,1)S(1)} %collective-permute-done.1.refs_2_, bf16[24,1024]{1,0:T(8,128)(2,1)S(1)} %collective-permute-done.2.refs_3_, ...), custom_call_target="tpu_custom_call" | custom-call | flops 503316480 | bytes 10485760 | tf_op jit(solution)/shard_map/pallas_call | solution.py:33
  19.4 0.0 copy-start.3
  19.4 0.0 copy-start.4
  19.4 0.6 %collective-permute-done.7.refs_2_ = f32[48,192]{1,0:T(8,128)S(1)} collective-permute-done((f32[48,192]{1,0:T(8,128)S(1)}, f32[48,192]{1,0:T(8,128)S(1)}, u32[]{:S(2)}, u32[]{:S(2)}) %collective-permute-start.7) | collective-permute-done | bytes 36896 | tf_op jit(solution)/shard_map/ppermute | solution.py:350
  20.0 0.5 %collective-permute-done.6.refs_1_ = f32[48,192]{1,0:T(8,128)S(1)} collective-permute-done((f32[48,192]{1,0:T(8,128)S(1)}, f32[48,192]{1,0:T(8,128)S(1)}, u32[]{:S(2)}, u32[]{:S(2)}) %collective-permute-start.6) | collective-permute-done | bytes 36896 | tf_op jit(solution)/shard_map/ppermute | solution.py:350
  20.6 0.8 %shard_map.121 = (f32[240,128]{1,0:T(8,128)S(1)}, s16[256,128]{1,0:T(8,128)(2,1)S(1)}, s16[256,128]{1,0:T(8,128)(2,1)S(1)}, s16[256,128]{1,0:T(8,128)(2,1)S(1)}) custom-call(f32[48,2560]{1,0:T(8,128)S(1)} %shard_map.119.base, f32[48,128]{1,0:T(8,128)S(1)} %get-tuple-element.24.ids, f32[48,192]{1,0:T(8,128)S(1)} %get-tuple-element.25.refs_0_, ...), custom_call_target="tpu_custom_call" | custom-call | flops 125829120 | bytes 2621440 | tf_op jit(solution)/shard_map/pallas_call | solution.py:33
  21.4 0.5 %collective-permute-start.9 = (s16[256,128]{1,0:T(8,128)(2,1)S(1)}, s16[256,128]{1,0:T(8,128)(2,1)S(1)}, u32[]{:S(2)}, u32[]{:S(2)}) collective-permute-start(s16[256,128]{1,0:T(8,128)(2,1)S(1)} %get-tuple-element.30), channel_id=1, source_target_pairs={{0,8},{4,12},{8,0},{12,4},{1,9},{5,13},{9,1},{13,5},{2,10},{6,14},... | collective-permute-start | bytes 196616 | tf_op jit(solution)/shard_map/ppermute | solution.py:376
  21.9 2.1 %collective-permute-start.10 = (s16[256,128]{1,0:T(8,128)(2,1)S(1)}, s16[256,128]{1,0:T(8,128)(2,1)S(1)}, u32[]{:S(2)}, u32[]{:S(2)}) collective-permute-start(s16[256,128]{1,0:T(8,128)(2,1)S(1)} %get-tuple-element.31), channel_id=1, source_target_pairs={{0,12},{4,8},{8,4},{12,0},{1,13},{5,9},{9,5},{13,1},{2,14},{6,10},... | collective-permute-start | bytes 196616 | tf_op jit(solution)/shard_map/ppermute | solution.py:376
  24.0 1.0 %collective-permute-start.11 = (s16[256,128]{1,0:T(8,128)(2,1)S(1)}, s16[256,128]{1,0:T(8,128)(2,1)S(1)}, u32[]{:S(2)}, u32[]{:S(2)}) collective-permute-start(s16[256,128]{1,0:T(8,128)(2,1)S(1)} %get-tuple-element.32), channel_id=1, source_target_pairs={{0,4},{4,0},{8,12},{12,8},{1,5},{5,1},{9,13},{13,9},{2,6},{6,2},{1... | collective-permute-start | bytes 196616 | tf_op jit(solution)/shard_map/ppermute | solution.py:376
  24.9 0.7 %shard_map.122 = (f32[216,128]{1,0:T(8,128)S(1)}, f32[216,128]{1,0:T(8,128)S(1)}, f32[12,192]{1,0:T(8,128)S(1)}) custom-call(s32[12]{0:T(128)} %lengths_far.1, f32[240,128]{1,0:T(8,128)S(1)} %get-tuple-element.26.after.refs_0_), custom_call_target="tpu_custom_call" | custom-call | tf_op jit(solution)/shard_map/pallas_call | solution.py:33
  25.7 2.9 %collective-permute-done.9.refs_1_ = s16[256,128]{1,0:T(8,128)(2,1)S(1)} collective-permute-done((s16[256,128]{1,0:T(8,128)(2,1)S(1)}, s16[256,128]{1,0:T(8,128)(2,1)S(1)}, u32[]{:S(2)}, u32[]{:S(2)}) %collective-permute-start.9) | collective-permute-done | bytes 65568 | tf_op jit(solution)/shard_map/ppermute | solution.py:376
  28.6 0.0 collective-permute-done.10.refs_2_
  28.6 0.5 %collective-permute-done.11.refs_3_ = s16[256,128]{1,0:T(8,128)(2,1)S(1)} collective-permute-done((s16[256,128]{1,0:T(8,128)(2,1)S(1)}, s16[256,128]{1,0:T(8,128)(2,1)S(1)}, u32[]{:S(2)}, u32[]{:S(2)}) %collective-permute-start.11) | collective-permute-done | bytes 65568 | tf_op jit(solution)/shard_map/ppermute | solution.py:376
  29.1 1.9 %shard_map.123 = bf16[12,2048]{1,0:T(8,128)(2,1)} custom-call(f32[12,192]{1,0:T(8,128)S(1)} %get-tuple-element.27.visible, f32[216,128]{1,0:T(8,128)S(1)} %get-tuple-element.28.cosine, f32[216,128]{1,0:T(8,128)S(1)} %get-tuple-element.29.sine, f32[240,128]{1,0:T(8,128)S(1)} %get-tuple-element.26.after.refs_0_, ...), custom_call_target="tpu_custom_call" | custom-call | flops 18874368 | bytes 2359296 | tf_op jit(solution)/shard_map/pallas_call | solution.py:33
  (14 shorter events, 0.0 us)
Async XLA Ops:
  0.0 13.2 %copy-start.1 = (bf16[8,3,64,2048]{3,2,1,0:T(8,128)(2,1)S(1)}, bf16[8,3,64,2048]{3,2,1,0:T(8,128)(2,1)}, u32[]{:S(2)}) copy-start(bf16[8,3,64,2048]{3,2,1,0:T(8,128)(2,1)} %param.21) | copy-start | bytes 18874372
  0.0 17.5 %copy-start = (bf16[2048,2048]{1,0:T(8,128)(2,1)S(1)}, bf16[2048,2048]{1,0:T(8,128)(2,1)}, u32[]{:S(2)}) copy-start(bf16[2048,2048]{1,0:T(8,128)(2,1)} %refs_4_.2) | copy-start | bytes 25165828
  1.5 10.1 %collective-permute-start.5 = (bf16[24,1152]{1,0:T(8,128)(2,1)S(1)}, bf16[24,1152]{1,0:T(8,128)(2,1)S(1)}, u32[]{:S(2)}, u32[]{:S(2)}) collective-permute-start(bf16[24,1152]{1,0:T(8,128)(2,1)S(1)} %get-tuple-element.23.refs_0_), channel_id=1, source_target_pairs={{0,12},{4,8},{8,4},{12,0},{1,13},{5,9},{9,5},{13,1},{2,14},{6,10},... | collective-permute-start | bytes 165896 | tf_op jit(solution)/shard_map/ppermute | solution.py:335
  6.6 6.6 %collective-permute-start.4 = (bf16[24,1152]{1,0:T(8,128)(2,1)S(1)}, bf16[24,1152]{1,0:T(8,128)(2,1)S(1)}, u32[]{:S(2)}, u32[]{:S(2)}) collective-permute-start(bf16[24,1152]{1,0:T(8,128)(2,1)S(1)} %get-tuple-element.23.refs_0_), channel_id=1, source_target_pairs={{0,8},{4,12},{8,0},{12,4},{1,9},{5,13},{9,1},{13,5},{2,10},{6,14},... | collective-permute-start | bytes 165896 | tf_op jit(solution)/shard_map/ppermute | solution.py:335
  6.6 6.6 %collective-permute-start.3 = (bf16[24,1152]{1,0:T(8,128)(2,1)S(1)}, bf16[24,1152]{1,0:T(8,128)(2,1)S(1)}, u32[]{:S(2)}, u32[]{:S(2)}) collective-permute-start(bf16[24,1152]{1,0:T(8,128)(2,1)S(1)} %get-tuple-element.23.refs_0_), channel_id=1, source_target_pairs={{0,4},{4,0},{8,12},{12,8},{1,5},{5,1},{9,13},{13,9},{2,6},{6,2},{1... | collective-permute-start | bytes 165896 | tf_op jit(solution)/shard_map/ppermute | solution.py:335
  7.3 9.7 %collective-permute-start = (bf16[24,1024]{1,0:T(8,128)(2,1)S(1)}, bf16[24,1024]{1,0:T(8,128)(2,1)S(1)}, u32[]{:S(2)}, u32[]{:S(2)}) collective-permute-start(bf16[24,1024]{1,0:T(8,128)(2,1)S(1)} %get-tuple-element.20), channel_id=1, source_target_pairs={{0,4},{4,0},{8,12},{12,8},{1,5},{5,1},{9,13},{13,9},{2,6},{6,2},{1... | collective-permute-start | bytes 147464 | tf_op jit(solution)/shard_map/ppermute | solution.py:338
  8.7 8.5 %collective-permute-start.1 = (bf16[24,1024]{1,0:T(8,128)(2,1)S(1)}, bf16[24,1024]{1,0:T(8,128)(2,1)S(1)}, u32[]{:S(2)}, u32[]{:S(2)}) collective-permute-start(bf16[24,1024]{1,0:T(8,128)(2,1)S(1)} %get-tuple-element.21), channel_id=1, source_target_pairs={{0,8},{4,12},{8,0},{12,4},{1,9},{5,13},{9,1},{13,5},{2,10},{6,14},... | collective-permute-start | bytes 147464 | tf_op jit(solution)/shard_map/ppermute | solution.py:338
  11.6 5.9 %collective-permute-start.2 = (bf16[24,1024]{1,0:T(8,128)(2,1)S(1)}, bf16[24,1024]{1,0:T(8,128)(2,1)S(1)}, u32[]{:S(2)}, u32[]{:S(2)}) collective-permute-start(bf16[24,1024]{1,0:T(8,128)(2,1)S(1)} %get-tuple-element.22), channel_id=1, source_target_pairs={{0,12},{4,8},{8,4},{12,0},{1,13},{5,9},{9,5},{13,1},{2,14},{6,10},... | collective-permute-start | bytes 147464 | tf_op jit(solution)/shard_map/ppermute | solution.py:338
  13.2 4.2 %copy-start.5 = (bf16[2048,256]{1,0:T(8,128)(2,1)S(1)}, bf16[2048,256]{1,0:T(8,128)(2,1)}, u32[]{:S(2)}) copy-start(bf16[2048,256]{1,0:T(8,128)(2,1)} %refs_5_.3) | copy-start | bytes 3145732
  13.3 4.2 %copy-start.6 = (bf16[2048,256]{1,0:T(8,128)(2,1)S(1)}, bf16[2048,256]{1,0:T(8,128)(2,1)}, u32[]{:S(2)}) copy-start(bf16[2048,256]{1,0:T(8,128)(2,1)} %refs_6_.1) | copy-start | bytes 3145732
  15.4 4.1 %collective-permute-start.8 = (f32[48,192]{1,0:T(8,128)S(1)}, f32[48,192]{1,0:T(8,128)S(1)}, u32[]{:S(2)}, u32[]{:S(2)}) collective-permute-start(f32[48,192]{1,0:T(8,128)S(1)} %get-tuple-element.25.refs_0_), channel_id=1, source_target_pairs={{0,3},{1,0},{2,1},{3,2},{4,7},{5,4},{6,5},{7,6},{8,11},{9,8},{10,9... | collective-permute-start | bytes 110600 | tf_op jit(solution)/shard_map/ppermute | solution.py:350
  15.4 4.6 %collective-permute-start.7 = (f32[48,192]{1,0:T(8,128)S(1)}, f32[48,192]{1,0:T(8,128)S(1)}, u32[]{:S(2)}, u32[]{:S(2)}) collective-permute-start(f32[48,192]{1,0:T(8,128)S(1)} %get-tuple-element.25.refs_0_), channel_id=1, source_target_pairs={{0,2},{1,3},{2,0},{3,1},{4,6},{5,7},{6,4},{7,5},{8,10},{9,11},{10,... | collective-permute-start | bytes 110600 | tf_op jit(solution)/shard_map/ppermute | solution.py:350
  17.0 3.6 %collective-permute-start.6 = (f32[48,192]{1,0:T(8,128)S(1)}, f32[48,192]{1,0:T(8,128)S(1)}, u32[]{:S(2)}, u32[]{:S(2)}) collective-permute-start(f32[48,192]{1,0:T(8,128)S(1)} %get-tuple-element.25.refs_0_), channel_id=1, source_target_pairs={{0,1},{1,2},{2,3},{3,0},{4,5},{5,6},{6,7},{7,4},{8,9},{9,10},{10,1... | collective-permute-start | bytes 110600 | tf_op jit(solution)/shard_map/ppermute | solution.py:350
  17.5 3.1 %copy-start.2 = (bf16[8,64,2048]{2,1,0:T(8,128)(2,1)S(1)}, bf16[8,64,2048]{2,1,0:T(8,128)(2,1)}, u32[]{:S(2)}) copy-start(bf16[8,64,2048]{2,1,0:T(8,128)(2,1)} %param.22) | copy-start | bytes 6291460
  17.5 3.1 %copy-start.7 = (bf16[8,2,64,256]{3,2,1,0:T(8,128)(2,1)S(1)}, bf16[8,2,64,256]{3,2,1,0:T(8,128)(2,1)}, u32[]{:S(2)}) copy-start(bf16[8,2,64,256]{3,2,1,0:T(8,128)(2,1)} %refs_5_.4) | copy-start | bytes 1572868
  19.4 9.7 %copy-start.3 = (bf16[12,2,192,128]{3,2,1,0:T(8,128)(2,1)S(1)}, bf16[12,2,192,128]{3,2,1,0:T(8,128)(2,1)}, u32[]{:S(2)}) copy-start(bf16[12,2,192,128]{3,2,1,0:T(8,128)(2,1)} %refs_4_.3) | copy-start | bytes 3538948
  19.4 9.7 %copy-start.4 = (bf16[12,2,192,128]{3,2,1,0:T(8,128)(2,1)S(1)}, bf16[12,2,192,128]{3,2,1,0:T(8,128)(2,1)}, u32[]{:S(2)}) copy-start(bf16[12,2,192,128]{3,2,1,0:T(8,128)(2,1)} %refs_5_.5) | copy-start | bytes 3538948
  21.4 7.2 %collective-permute-start.9 = (s16[256,128]{1,0:T(8,128)(2,1)S(1)}, s16[256,128]{1,0:T(8,128)(2,1)S(1)}, u32[]{:S(2)}, u32[]{:S(2)}) collective-permute-start(s16[256,128]{1,0:T(8,128)(2,1)S(1)} %get-tuple-element.30), channel_id=1, source_target_pairs={{0,8},{4,12},{8,0},{12,4},{1,9},{5,13},{9,1},{13,5},{2,10},{6,14},... | collective-permute-start | bytes 196616 | tf_op jit(solution)/shard_map/ppermute | solution.py:376
  21.9 6.7 %collective-permute-start.10 = (s16[256,128]{1,0:T(8,128)(2,1)S(1)}, s16[256,128]{1,0:T(8,128)(2,1)S(1)}, u32[]{:S(2)}, u32[]{:S(2)}) collective-permute-start(s16[256,128]{1,0:T(8,128)(2,1)S(1)} %get-tuple-element.31), channel_id=1, source_target_pairs={{0,12},{4,8},{8,4},{12,0},{1,13},{5,9},{9,5},{13,1},{2,14},{6,10},... | collective-permute-start | bytes 196616 | tf_op jit(solution)/shard_map/ppermute | solution.py:376
  24.0 5.1 %collective-permute-start.11 = (s16[256,128]{1,0:T(8,128)(2,1)S(1)}, s16[256,128]{1,0:T(8,128)(2,1)S(1)}, u32[]{:S(2)}, u32[]{:S(2)}) collective-permute-start(s16[256,128]{1,0:T(8,128)(2,1)S(1)} %get-tuple-element.32), channel_id=1, source_target_pairs={{0,4},{4,0},{8,12},{12,8},{1,5},{5,1},{9,13},{13,9},{2,6},{6,2},{1... | collective-permute-start | bytes 196616 | tf_op jit(solution)/shard_map/ppermute | solution.py:376

commit v3 on v2

--- a/solution.py
+++ b/solution.py
@@ -84,13 +84,13 @@
         ids = jnp.where((row == r) | (row == r + rows), index[r].astype(f32), ids)
     message[:, half:] = ids.astype(bf16)
     for k in range(wide):
-        target = lax.bitwise_xor(wide_place, k)
+        target = lax.rem(wide_place + k, wide)
         slices[k][...] = stacked(target * (2 * wide_half), wide_half)
 
 
-def joined(blocks):
-    rows = blocks[0].shape[0] // 2
-    values = [block[...].astype(f32) for block in blocks]
+def joined(own, *others):
+    rows = own.shape[0] // 2
+    values = [block[...].astype(f32) for block in (own, *reversed(others))]
     upper = jnp.concatenate([value[:rows] for value in values], axis=0)
     lower = jnp.concatenate([value[rows:] for value in values], axis=0)
     return upper, lower
@@ -100,28 +100,33 @@
     blocks, down, (sums, ids) = refs[:wide], refs[wide], refs[wide + 1 :]
     wide_place, _ = own_place()
     count = down.shape[0] // rank3
-    upper, lower = joined(blocks)
+    upper, lower = joined(*blocks)
     half = upper.shape[1] - LANES
     row_ids = upper[:, half:]
     ids[...] = row_ids
     features = jnp.concatenate([upper[:, :half], lower[:, :half]], axis=1).astype(bf16)
     first = wide_place * count
-    total = jnp.zeros((features.shape[0], rank3), f32)
+    column_ids = jnp.transpose(row_ids)[:1, :]
+    total = jnp.zeros((rank3, features.shape[0]), f32)
     for e in range(count):
         product = lax.dot_general(
+            down[e * rank3 : (e + 1) * rank3, :],
             features,
-            down[e * rank3 : (e + 1) * rank3, :],
             (((1,), (1,)), ((), ())),
             preferred_element_type=f32,
         )
-        total = jnp.where(row_ids[:, :1] == (first + e).astype(f32), product, total)
-    sums[...] = total
+        total = jnp.where(column_ids == (first + e).astype(f32), product, total)
+    rank2, half_rows = 2 * rank3 // 3, features.shape[0] // 2
+    sums[: 2 * half_rows, :] = jnp.transpose(total[:rank2])
+    sums[2 * half_rows :, :] = jnp.transpose(
+        jnp.concatenate([total[rank2:, :half_rows], total[rank2:, half_rows:]], axis=0)
+    )
 
 
 def base_kernel(wide, *refs):
     blocks, sources, out = refs[:wide], refs[wide:-1], refs[-1]
     chunk = 256
-    upper, lower = (part.astype(bf16) for part in joined(blocks))
+    upper, lower = (part.astype(bf16) for part in joined(*blocks))
     half = upper.shape[1]
     offset = 0
     for source in sources:
@@ -152,14 +157,19 @@
     total = parts[0][...]
     for part in parts[1:]:
         total = total + part[...]
-    rank_sums = total.astype(bf16)
+    rank_sums = total.astype(bf16).astype(f32)
+    last = rank_sums[all_rows:]
+    pieces = (
+        rank_sums[:all_rows, :rank],
+        rank_sums[:all_rows, rank:],
+        jnp.concatenate([last[:, :rank], last[:, rank:]], axis=0),
+    )
     row_ids = ids[:, :1]
     first = wide_place * count
 
     def widen(p):
-        piece = rank_sums[:, p * rank : (p + 1) * rank].astype(f32)
         return jnp.concatenate(
-            [jnp.where(row_ids == (first + e).astype(f32), piece, 0.0) for e in range(count)],
+            [jnp.where(row_ids == (first + e).astype(f32), pieces[p], 0.0) for e in range(count)],
             axis=1,
         ).astype(bf16)
 
@@ -243,8 +253,9 @@
     weights = jnp.exp(score - row_max)
     own_weight = jnp.exp(own - row_max)
     denominator = jnp.sum(weights, axis=-1, keepdims=True) + own_weight
-    weights = (weights / denominator).astype(bf16)
-    own_weight = (own_weight / denominator).astype(bf16).astype(f32)
+    share = 1.0 / denominator
+    weights = (weights * share).astype(bf16)
+    own_weight = (own_weight * share).astype(bf16).astype(f32)
     mixed = []
     for i, (r, g) in enumerate(pairs):
         new_value = rotated[pl.ds((heads + kv_heads + g) * rows + r, 1), :]
@@ -284,10 +295,6 @@
 
 def shifted(count, k):
     return [(i, (i + k) % count) for i in range(count)]
-
-
-def paired(count, k):
-    return [(i, i ^ k) for i in range(count)]
 
 
 def on_device(
@@ -331,18 +338,18 @@
         ],
         flops=10**10,
     )
-    blocks = [message] + [
-        lax.ppermute(message, "wide", paired(wide, k)) for k in range(1, wide)
+    blocks = [
+        lax.ppermute(message, "wide", shifted(wide, k)) for k in range(wide - 1, 0, -1)
     ]
-    wide_blocks = [slices[0]] + [
-        lax.ppermute(slices[k], "wide", paired(wide, k)) for k in range(1, wide)
+    wide_blocks = [
+        lax.ppermute(slices[k], "wide", shifted(wide, k)) for k in range(wide - 1, 0, -1)
     ]
     down = adapter_down_weight.reshape(count * rank3, slice_width)
     sums, ids = call(
         functools.partial(down_kernel, wide, rank3),
-        [shape_of((all_rows, rank3), f32), shape_of((all_rows, LANES), f32)],
+        [shape_of((all_rows * 3 // 2, 2 * rank), f32), shape_of((all_rows, LANES), f32)],
         [VMEM] * wide + [VMEM],
-        (*blocks, down),
+        (message, *blocks, down),
         vmem=12,
         flops=2 * all_rows * down.size,
         nbytes=2 * down.size,
@@ -353,7 +360,7 @@
         functools.partial(base_kernel, wide),
         shape_of((all_rows, width), f32),
         [VMEM] * wide + [VMEM] * 3,
-        (*wide_blocks, *weights),
+        (slices[0], *wide_blocks, *weights),
         vmem=16,
         flops=4 * all_rows * width * wide_half,
         nbytes=4 * width * wide_half,
@@ -373,7 +380,7 @@
         nbytes=2 * width * count * rank,
     )
     gathered = [outs[0]] + [
-        lax.ppermute(outs[k], "wide", paired(wide, k))
+        lax.ppermute(outs[k], "wide", shifted(wide, -k))
         for k in (LAST_ORDER if wide == 4 else range(1, wide))
     ]
     turned = (heads + kv_heads) * rows
@@ -391,7 +398,7 @@
         (visible, cosine, sine, *gathered, paged_key_cache, paged_value_cache),
         [
             pltpu.VMEM((body, LANES), f32),
-            pltpu.VMEM((heads * rows, LANES), f32),
+            pltpu.VMEM((heads * rows + 2 * STEP_ROWS, LANES), f32),
         ],
         vmem=8 + wide // 4,
         flops=4 * paged_key_cache.size * 8,

time: 31.2 us -> 30.4 us (0.974)
  starting transfers between devices: 17.1 us -> 16.7 us
    ppermute x3, waiting for transfers between devices: 1.12 us -> 0.01 us  [on_device(): lax.ppermute(sums, 'narrow', shifted(narrow, k))]
    ppermute x9, waiting for transfers between devices: 3.72 us -> 4.61 us  [the longest x3 2.42 us: on_device(): lax.ppermute(outs[k], 'wide', shifted(wide, -k))]
    ppermute x9, starting transfers between devices: 15.3 us -> 14.9 us  [the longest x3 7.01 us: on_device(): lax.ppermute(message, 'wide', shifted(wide, k))]
  transfers between devices with their start and end apart: 12 -> 12, of which waited for: 5 -> 7; matrix products, arithmetic and copies ran while one was open for 0% -> 0% of each run, Pallas kernels for 15% -> 15%
where the time goes in v3:
time: 30.4 us; the launch traced here: 30.2 us
  starting transfers between devices  16.7 us (55%)
  Pallas kernels  8.76 us (29%)
  waiting for transfers between devices  4.62 us (15%)
    pallas_call x6, Pallas kernels, call(): pl.pallas_call(kernel, out_shape=outs, in_specs=in_specs, out_specs=jax.t...  8.76 us
    ppermute x3, starting transfers between devices, on_device(): lax.ppermute(message, 'wide', shifted(wide, k))  7.01 us
    ppermute x3, starting transfers between devices, on_device(): lax.ppermute(outs[k], 'wide', shifted(wide, -k))  5.71 us
    ppermute x3, waiting for transfers between devices, on_device(): lax.ppermute(outs[k], 'wide', shifted(wide, -k))  2.42 us
    ppermute x3, starting transfers between devices, on_device(): lax.ppermute(slices[k], 'wide', shifted(wide, k))  2.22 us
    ppermute x3, starting transfers between devices, on_device(): lax.ppermute(sums, 'narrow', shifted(narrow, k))  1.73 us
    ppermute x3, waiting for transfers between devices, on_device(): lax.ppermute(slices[k], 'wide', shifted(wide, k))  1.27 us
    ppermute x3, waiting for transfers between devices, on_device(): lax.ppermute(message, 'wide', shifted(wide, k))  0.93 us
  transfers between devices with their start and end apart: 12, of which 7 were waited for; matrix products, arithmetic and copies ran while one was open for 0% of the time, Pallas kernels for 15%

profile of v3, /device:TPU:0, one launch (start us, length us, event | category | flops | bytes accessed | tf_op | source)
XLA Modules:
  0.0 30.2 jit_solution(5992430842226039975)
XLA Ops:
  0.0 1.5 %shard_map.118 = (bf16[24,1152]{1,0:T(8,128)(2,1)S(1)}, bf16[24,1024]{1,0:T(8,128)(2,1)S(1)}, bf16[24,1024]{1,0:T(8,128)(2,1)S(1)}, bf16[24,1024]{1,0:T(8,128)(2,1)S(1)}, bf16[24,1024]{1,0:T(8,128)(2,1)S(1)}) custom-call(s32[12]{0:T(128)} %index_far.1, bf16[12,8192]{1,0:T(8,128)(2,1)} %hidden_far.1, bf16[8192]{0:T(1024)(128)(2,1)} %gain_far.1), custom_call_target="tpu_custom_call" | custom-call | flops 10000000000 | tf_op jit(solution)/shard_map/pallas_call | solution.py:33
  1.5 3.1 %collective-permute-start.5 = (bf16[24,1152]{1,0:T(8,128)(2,1)S(1)}, bf16[24,1152]{1,0:T(8,128)(2,1)S(1)}, u32[]{:S(2)}, u32[]{:S(2)}) collective-permute-start(bf16[24,1152]{1,0:T(8,128)(2,1)S(1)} %get-tuple-element.23.refs_0_), channel_id=1, source_target_pairs={{0,4},{4,8},{8,12},{12,0},{1,5},{5,9},{9,13},{13,1},{2,6},{6,10},{... | collective-permute-start | bytes 165896 | tf_op jit(solution)/shard_map/ppermute | solution.py:342
  4.6 2.6 %collective-permute-start.4 = (bf16[24,1152]{1,0:T(8,128)(2,1)S(1)}, bf16[24,1152]{1,0:T(8,128)(2,1)S(1)}, u32[]{:S(2)}, u32[]{:S(2)}) collective-permute-start(bf16[24,1152]{1,0:T(8,128)(2,1)S(1)} %get-tuple-element.23.refs_0_), channel_id=1, source_target_pairs={{0,8},{4,12},{8,0},{12,4},{1,9},{5,13},{9,1},{13,5},{2,10},{6,14},... | collective-permute-start | bytes 165896 | tf_op jit(solution)/shard_map/ppermute | solution.py:342
  7.2 1.3 %collective-permute-start.3 = (bf16[24,1152]{1,0:T(8,128)(2,1)S(1)}, bf16[24,1152]{1,0:T(8,128)(2,1)S(1)}, u32[]{:S(2)}, u32[]{:S(2)}) collective-permute-start(bf16[24,1152]{1,0:T(8,128)(2,1)S(1)} %get-tuple-element.23.refs_0_), channel_id=1, source_target_pairs={{0,12},{4,0},{8,4},{12,8},{1,13},{5,1},{9,5},{13,9},{2,14},{6,2},{... | collective-permute-start | bytes 165896 | tf_op jit(solution)/shard_map/ppermute | solution.py:342
  8.5 0.4 %collective-permute-start = (bf16[24,1024]{1,0:T(8,128)(2,1)S(1)}, bf16[24,1024]{1,0:T(8,128)(2,1)S(1)}, u32[]{:S(2)}, u32[]{:S(2)}) collective-permute-start(bf16[24,1024]{1,0:T(8,128)(2,1)S(1)} %get-tuple-element.20), channel_id=1, source_target_pairs={{0,12},{4,0},{8,4},{12,8},{1,13},{5,1},{9,5},{13,9},{2,14},{6,2},{... | collective-permute-start | bytes 147464 | tf_op jit(solution)/shard_map/ppermute | solution.py:345
  9.0 1.7 %collective-permute-start.1 = (bf16[24,1024]{1,0:T(8,128)(2,1)S(1)}, bf16[24,1024]{1,0:T(8,128)(2,1)S(1)}, u32[]{:S(2)}, u32[]{:S(2)}) collective-permute-start(bf16[24,1024]{1,0:T(8,128)(2,1)S(1)} %get-tuple-element.21), channel_id=1, source_target_pairs={{0,8},{4,12},{8,0},{12,4},{1,9},{5,13},{9,1},{13,5},{2,10},{6,14},... | collective-permute-start | bytes 147464 | tf_op jit(solution)/shard_map/ppermute | solution.py:345
  10.7 0.0 collective-permute-done.5.refs_3_
  10.7 0.1 collective-permute-start.2
  10.7 0.2 collective-permute-done.4.refs_2_
  11.0 0.7 %collective-permute-done.3.refs_1_ = bf16[24,1152]{1,0:T(8,128)(2,1)S(1)} collective-permute-done((bf16[24,1152]{1,0:T(8,128)(2,1)S(1)}, bf16[24,1152]{1,0:T(8,128)(2,1)S(1)}, u32[]{:S(2)}, u32[]{:S(2)}) %collective-permute-start.3) | collective-permute-done | bytes 55328 | tf_op jit(solution)/shard_map/ppermute | solution.py:342
  11.7 1.9 %shard_map.120 = (f32[72,128]{1,0:T(8,128)S(1)}, f32[48,128]{1,0:T(8,128)S(1)}) custom-call(bf16[24,1152]{1,0:T(8,128)(2,1)S(1)} %get-tuple-element.23.refs_0_, bf16[24,1152]{1,0:T(8,128)(2,1)S(1)} %collective-permute-done.3.refs_1_, bf16[24,1152]{1,0:T(8,128)(2,1)S(1)} %collective-permute-done.4.refs_2_, ...), custom_call_target="tpu_custom_call" | custom-call | flops 301989888 | bytes 6291456 | tf_op jit(solution)/shard_map/pallas_call | solution.py:33
  13.5 0.1 collective-permute-start.8
  13.6 1.5 %collective-permute-start.7 = (f32[72,128]{1,0:T(8,128)S(1)}, f32[72,128]{1,0:T(8,128)S(1)}, u32[]{:S(2)}, u32[]{:S(2)}) collective-permute-start(f32[72,128]{1,0:T(8,128)S(1)} %get-tuple-element.25.refs_0_), channel_id=1, source_target_pairs={{0,2},{1,3},{2,0},{3,1},{4,6},{5,7},{6,4},{7,5},{8,10},{9,11},{10,... | collective-permute-start | bytes 110600 | tf_op jit(solution)/shard_map/ppermute | solution.py:357
  15.1 0.2 collective-permute-start.6
  15.3 0.4 %collective-permute-done.1.refs_2_ = bf16[24,1024]{1,0:T(8,128)(2,1)S(1)} collective-permute-done((bf16[24,1024]{1,0:T(8,128)(2,1)S(1)}, bf16[24,1024]{1,0:T(8,128)(2,1)S(1)}, u32[]{:S(2)}, u32[]{:S(2)}) %collective-permute-start.1) | collective-permute-done | bytes 49184 | tf_op jit(solution)/shard_map/ppermute | solution.py:345
  15.7 0.8 %collective-permute-done.2.refs_3_ = bf16[24,1024]{1,0:T(8,128)(2,1)S(1)} collective-permute-done((bf16[24,1024]{1,0:T(8,128)(2,1)S(1)}, bf16[24,1024]{1,0:T(8,128)(2,1)S(1)}, u32[]{:S(2)}, u32[]{:S(2)}) %collective-permute-start.2) | collective-permute-done | bytes 49184 | tf_op jit(solution)/shard_map/ppermute | solution.py:345
  16.6 0.0 copy-start.2
  16.6 0.0 copy-start.7
  16.6 1.9 %shard_map.119.base = f32[48,2560]{1,0:T(8,128)S(1)} custom-call(bf16[24,1024]{1,0:T(8,128)(2,1)S(1)} %get-tuple-element.19.refs_0_, bf16[24,1024]{1,0:T(8,128)(2,1)S(1)} %collective-permute-done.refs_1_, bf16[24,1024]{1,0:T(8,128)(2,1)S(1)} %collective-permute-done.1.refs_2_, bf16[24,1024]{1,0:T(8,128)(2,1)S(1)} %collective-permute-done.2.refs_3_, ...), custom_call_target="tpu_custom_call" | custom-call | flops 503316480 | bytes 10485760 | tf_op jit(solution)/shard_map/pallas_call | solution.py:33
  18.5 0.0 copy-start.3
  18.5 0.0 copy-start.4
  18.5 0.0 collective-permute-done.8.refs_3_
  18.5 0.0 collective-permute-done.6.refs_1_
  18.6 0.8 %shard_map.121 = (f32[240,128]{1,0:T(8,128)S(1)}, s16[256,128]{1,0:T(8,128)(2,1)S(1)}, s16[256,128]{1,0:T(8,128)(2,1)S(1)}, s16[256,128]{1,0:T(8,128)(2,1)S(1)}) custom-call(f32[48,2560]{1,0:T(8,128)S(1)} %shard_map.119.base, f32[48,128]{1,0:T(8,128)S(1)} %get-tuple-element.24.ids, f32[72,128]{1,0:T(8,128)S(1)} %get-tuple-element.25.refs_0_, ...), custom_call_target="tpu_custom_call" | custom-call | flops 125829120 | bytes 2621440 | tf_op jit(solution)/shard_map/pallas_call | solution.py:33
  19.4 1.9 %collective-permute-start.9 = (s16[256,128]{1,0:T(8,128)(2,1)S(1)}, s16[256,128]{1,0:T(8,128)(2,1)S(1)}, u32[]{:S(2)}, u32[]{:S(2)}) collective-permute-start(s16[256,128]{1,0:T(8,128)(2,1)S(1)} %get-tuple-element.30), channel_id=1, source_target_pairs={{0,8},{4,12},{8,0},{12,4},{1,9},{5,13},{9,1},{13,5},{2,10},{6,14},... | collective-permute-start | bytes 196616 | tf_op jit(solution)/shard_map/ppermute | solution.py:383
  21.3 2.7 %collective-permute-start.10 = (s16[256,128]{1,0:T(8,128)(2,1)S(1)}, s16[256,128]{1,0:T(8,128)(2,1)S(1)}, u32[]{:S(2)}, u32[]{:S(2)}) collective-permute-start(s16[256,128]{1,0:T(8,128)(2,1)S(1)} %get-tuple-element.31), channel_id=1, source_target_pairs={{0,4},{4,8},{8,12},{12,0},{1,5},{5,9},{9,13},{13,1},{2,6},{6,10},{... | collective-permute-start | bytes 196616 | tf_op jit(solution)/shard_map/ppermute | solution.py:383
  24.0 1.1 %collective-permute-start.11 = (s16[256,128]{1,0:T(8,128)(2,1)S(1)}, s16[256,128]{1,0:T(8,128)(2,1)S(1)}, u32[]{:S(2)}, u32[]{:S(2)}) collective-permute-start(s16[256,128]{1,0:T(8,128)(2,1)S(1)} %get-tuple-element.32), channel_id=1, source_target_pairs={{0,12},{4,0},{8,4},{12,8},{1,13},{5,1},{9,5},{13,9},{2,14},{6,2},{... | collective-permute-start | bytes 196616 | tf_op jit(solution)/shard_map/ppermute | solution.py:383
  25.1 0.7 %shard_map.122 = (f32[216,128]{1,0:T(8,128)S(1)}, f32[216,128]{1,0:T(8,128)S(1)}, f32[12,192]{1,0:T(8,128)S(1)}) custom-call(s32[12]{0:T(128)} %lengths_far.1, f32[240,128]{1,0:T(8,128)S(1)} %get-tuple-element.26.after.refs_0_), custom_call_target="tpu_custom_call" | custom-call | tf_op jit(solution)/shard_map/pallas_call | solution.py:33
  25.9 0.3 collective-permute-done.9.refs_1_
  26.1 1.5 %collective-permute-done.10.refs_2_ = s16[256,128]{1,0:T(8,128)(2,1)S(1)} collective-permute-done((s16[256,128]{1,0:T(8,128)(2,1)S(1)}, s16[256,128]{1,0:T(8,128)(2,1)S(1)}, u32[]{:S(2)}, u32[]{:S(2)}) %collective-permute-start.10) | collective-permute-done | bytes 65568 | tf_op jit(solution)/shard_map/ppermute | solution.py:383
  27.6 0.7 %collective-permute-done.11.refs_3_ = s16[256,128]{1,0:T(8,128)(2,1)S(1)} collective-permute-done((s16[256,128]{1,0:T(8,128)(2,1)S(1)}, s16[256,128]{1,0:T(8,128)(2,1)S(1)}, u32[]{:S(2)}, u32[]{:S(2)}) %collective-permute-start.11) | collective-permute-done | bytes 65568 | tf_op jit(solution)/shard_map/ppermute | solution.py:383
  28.3 1.9 %shard_map.123 = bf16[12,2048]{1,0:T(8,128)(2,1)} custom-call(f32[12,192]{1,0:T(8,128)S(1)} %get-tuple-element.27.visible, f32[216,128]{1,0:T(8,128)S(1)} %get-tuple-element.28.cosine, f32[216,128]{1,0:T(8,128)S(1)} %get-tuple-element.29.sine, f32[240,128]{1,0:T(8,128)S(1)} %get-tuple-element.26.after.refs_0_, ...), custom_call_target="tpu_custom_call" | custom-call | flops 18874368 | bytes 2359296 | tf_op jit(solution)/shard_map/pallas_call | solution.py:33
  (14 shorter events, 0.0 us)
Async XLA Ops:
  0.0 11.7 %copy-start.1 = (bf16[8,3,64,2048]{3,2,1,0:T(8,128)(2,1)S(1)}, bf16[8,3,64,2048]{3,2,1,0:T(8,128)(2,1)}, u32[]{:S(2)}) copy-start(bf16[8,3,64,2048]{3,2,1,0:T(8,128)(2,1)} %param.21) | copy-start | bytes 18874372
  0.0 16.6 %copy-start = (bf16[2048,2048]{1,0:T(8,128)(2,1)S(1)}, bf16[2048,2048]{1,0:T(8,128)(2,1)}, u32[]{:S(2)}) copy-start(bf16[2048,2048]{1,0:T(8,128)(2,1)} %refs_4_.2) | copy-start | bytes 25165828
  1.5 9.2 %collective-permute-start.5 = (bf16[24,1152]{1,0:T(8,128)(2,1)S(1)}, bf16[24,1152]{1,0:T(8,128)(2,1)S(1)}, u32[]{:S(2)}, u32[]{:S(2)}) collective-permute-start(bf16[24,1152]{1,0:T(8,128)(2,1)S(1)} %get-tuple-element.23.refs_0_), channel_id=1, source_target_pairs={{0,4},{4,8},{8,12},{12,0},{1,5},{5,9},{9,13},{13,1},{2,6},{6,10},{... | collective-permute-start | bytes 165896 | tf_op jit(solution)/shard_map/ppermute | solution.py:342
  4.6 6.4 %collective-permute-start.4 = (bf16[24,1152]{1,0:T(8,128)(2,1)S(1)}, bf16[24,1152]{1,0:T(8,128)(2,1)S(1)}, u32[]{:S(2)}, u32[]{:S(2)}) collective-permute-start(bf16[24,1152]{1,0:T(8,128)(2,1)S(1)} %get-tuple-element.23.refs_0_), channel_id=1, source_target_pairs={{0,8},{4,12},{8,0},{12,4},{1,9},{5,13},{9,1},{13,5},{2,10},{6,14},... | collective-permute-start | bytes 165896 | tf_op jit(solution)/shard_map/ppermute | solution.py:342
  7.2 4.5 %collective-permute-start.3 = (bf16[24,1152]{1,0:T(8,128)(2,1)S(1)}, bf16[24,1152]{1,0:T(8,128)(2,1)S(1)}, u32[]{:S(2)}, u32[]{:S(2)}) collective-permute-start(bf16[24,1152]{1,0:T(8,128)(2,1)S(1)} %get-tuple-element.23.refs_0_), channel_id=1, source_target_pairs={{0,12},{4,0},{8,4},{12,8},{1,13},{5,1},{9,5},{13,9},{2,14},{6,2},{... | collective-permute-start | bytes 165896 | tf_op jit(solution)/shard_map/ppermute | solution.py:342
  8.5 6.6 %collective-permute-start = (bf16[24,1024]{1,0:T(8,128)(2,1)S(1)}, bf16[24,1024]{1,0:T(8,128)(2,1)S(1)}, u32[]{:S(2)}, u32[]{:S(2)}) collective-permute-start(bf16[24,1024]{1,0:T(8,128)(2,1)S(1)} %get-tuple-element.20), channel_id=1, source_target_pairs={{0,12},{4,0},{8,4},{12,8},{1,13},{5,1},{9,5},{13,9},{2,14},{6,2},{... | collective-permute-start | bytes 147464 | tf_op jit(solution)/shard_map/ppermute | solution.py:345
  9.0 6.8 %collective-permute-start.1 = (bf16[24,1024]{1,0:T(8,128)(2,1)S(1)}, bf16[24,1024]{1,0:T(8,128)(2,1)S(1)}, u32[]{:S(2)}, u32[]{:S(2)}) collective-permute-start(bf16[24,1024]{1,0:T(8,128)(2,1)S(1)} %get-tuple-element.21), channel_id=1, source_target_pairs={{0,8},{4,12},{8,0},{12,4},{1,9},{5,13},{9,1},{13,5},{2,10},{6,14},... | collective-permute-start | bytes 147464 | tf_op jit(solution)/shard_map/ppermute | solution.py:345
  10.7 5.9 %collective-permute-start.2 = (bf16[24,1024]{1,0:T(8,128)(2,1)S(1)}, bf16[24,1024]{1,0:T(8,128)(2,1)S(1)}, u32[]{:S(2)}, u32[]{:S(2)}) collective-permute-start(bf16[24,1024]{1,0:T(8,128)(2,1)S(1)} %get-tuple-element.22), channel_id=1, source_target_pairs={{0,4},{4,8},{8,12},{12,0},{1,5},{5,9},{9,13},{13,1},{2,6},{6,10},{... | collective-permute-start | bytes 147464 | tf_op jit(solution)/shard_map/ppermute | solution.py:345
  11.7 4.9 %copy-start.5 = (bf16[2048,256]{1,0:T(8,128)(2,1)S(1)}, bf16[2048,256]{1,0:T(8,128)(2,1)}, u32[]{:S(2)}) copy-start(bf16[2048,256]{1,0:T(8,128)(2,1)} %refs_5_.3) | copy-start | bytes 3145732
  11.7 4.9 %copy-start.6 = (bf16[2048,256]{1,0:T(8,128)(2,1)S(1)}, bf16[2048,256]{1,0:T(8,128)(2,1)}, u32[]{:S(2)}) copy-start(bf16[2048,256]{1,0:T(8,128)(2,1)} %refs_6_.1) | copy-start | bytes 3145732
  13.5 5.0 %collective-permute-start.8 = (f32[72,128]{1,0:T(8,128)S(1)}, f32[72,128]{1,0:T(8,128)S(1)}, u32[]{:S(2)}, u32[]{:S(2)}) collective-permute-start(f32[72,128]{1,0:T(8,128)S(1)} %get-tuple-element.25.refs_0_), channel_id=1, source_target_pairs={{0,3},{1,0},{2,1},{3,2},{4,7},{5,4},{6,5},{7,6},{8,11},{9,8},{10,9... | collective-permute-start | bytes 110600 | tf_op jit(solution)/shard_map/ppermute | solution.py:357
  13.6 4.9 %collective-permute-start.7 = (f32[72,128]{1,0:T(8,128)S(1)}, f32[72,128]{1,0:T(8,128)S(1)}, u32[]{:S(2)}, u32[]{:S(2)}) collective-permute-start(f32[72,128]{1,0:T(8,128)S(1)} %get-tuple-element.25.refs_0_), channel_id=1, source_target_pairs={{0,2},{1,3},{2,0},{3,1},{4,6},{5,7},{6,4},{7,5},{8,10},{9,11},{10,... | collective-permute-start | bytes 110600 | tf_op jit(solution)/shard_map/ppermute | solution.py:357
  15.1 3.4 %collective-permute-start.6 = (f32[72,128]{1,0:T(8,128)S(1)}, f32[72,128]{1,0:T(8,128)S(1)}, u32[]{:S(2)}, u32[]{:S(2)}) collective-permute-start(f32[72,128]{1,0:T(8,128)S(1)} %get-tuple-element.25.refs_0_), channel_id=1, source_target_pairs={{0,1},{1,2},{2,3},{3,0},{4,5},{5,6},{6,7},{7,4},{8,9},{9,10},{10,1... | collective-permute-start | bytes 110600 | tf_op jit(solution)/shard_map/ppermute | solution.py:357
  16.6 2.0 %copy-start.2 = (bf16[8,64,2048]{2,1,0:T(8,128)(2,1)S(1)}, bf16[8,64,2048]{2,1,0:T(8,128)(2,1)}, u32[]{:S(2)}) copy-start(bf16[8,64,2048]{2,1,0:T(8,128)(2,1)} %param.22) | copy-start | bytes 6291460
  16.6 2.0 %copy-start.7 = (bf16[8,2,64,256]{3,2,1,0:T(8,128)(2,1)S(1)}, bf16[8,2,64,256]{3,2,1,0:T(8,128)(2,1)}, u32[]{:S(2)}) copy-start(bf16[8,2,64,256]{3,2,1,0:T(8,128)(2,1)} %refs_5_.4) | copy-start | bytes 1572868
  18.5 9.8 %copy-start.3 = (bf16[12,2,192,128]{3,2,1,0:T(8,128)(2,1)S(1)}, bf16[12,2,192,128]{3,2,1,0:T(8,128)(2,1)}, u32[]{:S(2)}) copy-start(bf16[12,2,192,128]{3,2,1,0:T(8,128)(2,1)} %refs_4_.3) | copy-start | bytes 3538948
  18.5 9.8 %copy-start.4 = (bf16[12,2,192,128]{3,2,1,0:T(8,128)(2,1)S(1)}, bf16[12,2,192,128]{3,2,1,0:T(8,128)(2,1)}, u32[]{:S(2)}) copy-start(bf16[12,2,192,128]{3,2,1,0:T(8,128)(2,1)} %refs_5_.5) | copy-start | bytes 3538948
  19.4 6.7 %collective-permute-start.9 = (s16[256,128]{1,0:T(8,128)(2,1)S(1)}, s16[256,128]{1,0:T(8,128)(2,1)S(1)}, u32[]{:S(2)}, u32[]{:S(2)}) collective-permute-start(s16[256,128]{1,0:T(8,128)(2,1)S(1)} %get-tuple-element.30), channel_id=1, source_target_pairs={{0,8},{4,12},{8,0},{12,4},{1,9},{5,13},{9,1},{13,5},{2,10},{6,14},... | collective-permute-start | bytes 196616 | tf_op jit(solution)/shard_map/ppermute | solution.py:383
  21.3 6.3 %collective-permute-start.10 = (s16[256,128]{1,0:T(8,128)(2,1)S(1)}, s16[256,128]{1,0:T(8,128)(2,1)S(1)}, u32[]{:S(2)}, u32[]{:S(2)}) collective-permute-start(s16[256,128]{1,0:T(8,128)(2,1)S(1)} %get-tuple-element.31), channel_id=1, source_target_pairs={{0,4},{4,8},{8,12},{12,0},{1,5},{5,9},{9,13},{13,1},{2,6},{6,10},{... | collective-permute-start | bytes 196616 | tf_op jit(solution)/shard_map/ppermute | solution.py:383
  24.0 4.3 %collective-permute-start.11 = (s16[256,128]{1,0:T(8,128)(2,1)S(1)}, s16[256,128]{1,0:T(8,128)(2,1)S(1)}, u32[]{:S(2)}, u32[]{:S(2)}) collective-permute-start(s16[256,128]{1,0:T(8,128)(2,1)S(1)} %get-tuple-element.32), channel_id=1, source_target_pairs={{0,12},{4,0},{8,4},{12,8},{1,13},{5,1},{9,5},{13,9},{2,14},{6,2},{... | collective-permute-start | bytes 196616 | tf_op jit(solution)/shard_map/ppermute | solution.py:383

commit v4 on v3

--- a/solution.py
+++ b/solution.py
@@ -127,14 +127,14 @@
     blocks, sources, out = refs[:wide], refs[wide:-1], refs[-1]
     chunk = 256
     upper, lower = (part.astype(bf16) for part in joined(*blocks))
-    half = upper.shape[1]
+    features = jnp.concatenate([upper, lower], axis=1)
     offset = 0
     for source in sources:
         for start in range(0, source.shape[1], chunk):
             columns = slice(start, start + chunk)
             out[:, offset + start : offset + start + chunk] = jnp.dot(
-                upper, source[:half, columns], preferred_element_type=f32
-            ) + jnp.dot(lower, source[half:, columns], preferred_element_type=f32)
+                features, source[:, columns], preferred_element_type=f32
+            )
         offset += source.shape[1]
 
 
@@ -219,7 +219,7 @@
 
 def attend_kernel(wide, heads, kv_heads, visible, cosine, sine, *refs):
     parts, (keys, values, out, rotated, attended) = refs[:wide], refs[wide:]
-    rows, _, _, width = keys.shape
+    rows, _, width, _ = keys.shape
     group = heads // kv_heads
     body = (heads + 2 * kv_heads) * rows
     total = parts[0][...]
@@ -239,15 +239,25 @@
     rotated[turned:] = total[turned:].astype(bf16).astype(f32)
     factor = 1.0 / math.sqrt(width)
     pairs = [(r, g) for r in range(rows) for g in range(kv_heads)]
+    nothing = jnp.zeros((group, width), bf16)
     scores, own = [], []
-    for r, g in pairs:
-        query = rotated[pl.ds(g * group * rows + r, group, stride=rows), :]
-        new_key = rotated[pl.ds((heads + g) * rows + r, 1), :]
-        score = lax.dot_general(
-            query.astype(bf16), keys[r, g], (((1,), (1,)), ((), ())), preferred_element_type=f32
+    for r in range(rows):
+        spread = []
+        for g in range(kv_heads):
+            query = rotated[pl.ds(g * group * rows + r, group, stride=rows), :]
+            new_key = rotated[pl.ds((heads + g) * rows + r, 1), :]
+            own.append(jnp.sum(query * new_key, axis=-1, keepdims=True) * factor)
+            spread.append(
+                jnp.concatenate(
+                    [query.astype(bf16) if i == g else nothing for i in range(kv_heads)], axis=1
+                )
+            )
+        score = jnp.dot(
+            jnp.concatenate(spread, axis=0),
+            keys[r].reshape(kv_heads * width, keys.shape[3]),
+            preferred_element_type=f32,
         )
         scores.append(score * factor + visible[r : r + 1, :])
-        own.append(jnp.sum(query * new_key, axis=-1, keepdims=True) * factor)
     score, own = jnp.concatenate(scores, axis=0), jnp.concatenate(own, axis=0)
     row_max = jnp.maximum(jnp.max(score, axis=-1, keepdims=True), own)
     weights = jnp.exp(score - row_max)
@@ -257,20 +267,26 @@
     weights = (weights * share).astype(bf16)
     own_weight = (own_weight * share).astype(bf16).astype(f32)
     mixed = []
-    for i, (r, g) in enumerate(pairs):
-        new_value = rotated[pl.ds((heads + kv_heads + g) * rows + r, 1), :]
-        window = slice(i * group, (i + 1) * group)
-        mixed.append(
-            jnp.dot(weights[window], values[r, g], preferred_element_type=f32)
-            + own_weight[window] * new_value
-        )
+    for r in range(rows):
+        window = slice(r * kv_heads * group, (r + 1) * kv_heads * group)
+        both = jnp.dot(
+            weights[window],
+            jnp.concatenate([values[r, g] for g in range(kv_heads)], axis=1),
+            preferred_element_type=f32,
+        )
+        for g in range(kv_heads):
+            new_value = rotated[pl.ds((heads + kv_heads + g) * rows + r, 1), :]
+            place = slice(g * group, (g + 1) * group)
+            mixed.append(
+                both[place, g * width : (g + 1) * width] + own_weight[window][place] * new_value
+            )
     for i, (r, g) in enumerate(pairs):
         attended[pl.ds(g * group * rows + r, group, stride=rows), :] = mixed[i]
     for h in range(heads):
         out[:, h * width : (h + 1) * width] = attended[h * rows : (h + 1) * rows, :].astype(bf16)
 
 
-def rotation_kernel(lengths_far, after, cosine, sine, visible, lengths, sem):
+def ready_kernel(lengths_far, after, keys, cosine, sine, visible, turned_keys, lengths, sem):
     copy = pltpu.make_async_copy(lengths_far, lengths, sem)
     copy.start()
     rows, positions = visible.shape
@@ -291,6 +307,9 @@
     repeats = cosine.shape[0] // rows
     cosine[...] = jnp.concatenate([cosines] * repeats, axis=0)
     sine[...] = jnp.concatenate([sines] * repeats, axis=0)
+    for r in range(rows):
+        for g in range(keys.shape[1]):
+            turned_keys[r, g] = jnp.transpose(keys[r, g])
 
 
 def shifted(count, k):
@@ -384,18 +403,21 @@
         for k in (LAST_ORDER if wide == 4 else range(1, wide))
     ]
     turned = (heads + kv_heads) * rows
-    cosine, sine, visible = call(
-        rotation_kernel,
-        [shape_of((turned, LANES), f32)] * 2 + [shape_of((rows, paged_key_cache.shape[2]), f32)],
-        [HBM, ANY],
-        (pltpu.with_memory_space_constraint(lengths, pltpu.HBM), outs[0]),
+    positions = paged_key_cache.shape[2]
+    cosine, sine, visible, turned_keys = call(
+        ready_kernel,
+        [shape_of((turned, LANES), f32)] * 2
+        + [shape_of((rows, positions), f32)]
+        + [shape_of((rows, kv_heads, HEAD_WIDTH, positions), bf16)],
+        [HBM, ANY, VMEM],
+        (pltpu.with_memory_space_constraint(lengths, pltpu.HBM), outs[0], paged_key_cache),
         [pltpu.SMEM((rows,), jnp.int32), pltpu.SemaphoreType.DMA],
     )
     return call(
         functools.partial(attend_kernel, wide, heads, kv_heads),
         shape_of((rows, query_width), bf16),
         [VMEM] * (3 + wide + 2),
-        (visible, cosine, sine, *gathered, paged_key_cache, paged_value_cache),
+        (visible, cosine, sine, *gathered, turned_keys, paged_value_cache),
         [
             pltpu.VMEM((body, LANES), f32),
             pltpu.VMEM((heads * rows + 2 * STEP_ROWS, LANES), f32),

time: 30.4 us -> 30 us (0.987)
  waiting for transfers between devices: 4.62 us -> 4.18 us
    ppermute x3, waiting for transfers between devices: 2.42 us -> 1.98 us  [on_device(): lax.ppermute(outs[k], 'wide', shifted(wide, -k))]
  transfers between devices with their start and end apart: 12 -> 12, of which waited for: 7 -> 6; matrix products, arithmetic and copies ran while one was open for 0% -> 0% of each run, Pallas kernels for 15% -> 17%
where the time goes in v4:
time: 30 us; the launch traced here: 29.9 us
  starting transfers between devices  16.7 us (56%)
  Pallas kernels  8.84 us (29%)
  waiting for transfers between devices  4.18 us (14%)
    pallas_call x6, Pallas kernels, call(): pl.pallas_call(kernel, out_shape=outs, in_specs=in_specs, out_specs=jax.t...  8.84 us
    ppermute x3, starting transfers between devices, on_device(): lax.ppermute(message, 'wide', shifted(wide, k))  7.01 us
    ppermute x3, starting transfers between devices, on_device(): lax.ppermute(outs[k], 'wide', shifted(wide, -k))  5.71 us
    ppermute x3, starting transfers between devices, on_device(): lax.ppermute(slices[k], 'wide', shifted(wide, k))  2.22 us
    ppermute x3, waiting for transfers between devices, on_device(): lax.ppermute(outs[k], 'wide', shifted(wide, -k))  1.98 us
    ppermute x3, starting transfers between devices, on_device(): lax.ppermute(sums, 'narrow', shifted(narrow, k))  1.73 us
    ppermute x3, waiting for transfers between devices, on_device(): lax.ppermute(slices[k], 'wide', shifted(wide, k))  1.27 us
    ppermute x3, waiting for transfers between devices, on_device(): lax.ppermute(message, 'wide', shifted(wide, k))  0.93 us
  transfers between devices with their start and end apart: 12, of which 6 were waited for; matrix products, arithmetic and copies ran while one was open for 0% of the time, Pallas kernels for 17%

profile of v4, /device:TPU:0, one launch (start us, length us, event | category | flops | bytes accessed | tf_op | source)
XLA Modules:
  0.0 29.9 jit_solution(5648797411671335498)
XLA Ops:
  0.0 1.5 %shard_map.118 = (bf16[24,1152]{1,0:T(8,128)(2,1)S(1)}, bf16[24,1024]{1,0:T(8,128)(2,1)S(1)}, bf16[24,1024]{1,0:T(8,128)(2,1)S(1)}, bf16[24,1024]{1,0:T(8,128)(2,1)S(1)}, bf16[24,1024]{1,0:T(8,128)(2,1)S(1)}) custom-call(s32[12]{0:T(128)} %index_far.1, bf16[12,8192]{1,0:T(8,128)(2,1)} %hidden_far.1, bf16[8192]{0:T(1024)(128)(2,1)} %gain_far.1), custom_call_target="tpu_custom_call" | custom-call | flops 10000000000 | tf_op jit(solution)/shard_map/pallas_call | solution.py:33
  1.5 3.1 %collective-permute-start.5 = (bf16[24,1152]{1,0:T(8,128)(2,1)S(1)}, bf16[24,1152]{1,0:T(8,128)(2,1)S(1)}, u32[]{:S(2)}, u32[]{:S(2)}) collective-permute-start(bf16[24,1152]{1,0:T(8,128)(2,1)S(1)} %get-tuple-element.24.refs_0_), channel_id=1, source_target_pairs={{0,4},{4,8},{8,12},{12,0},{1,5},{5,9},{9,13},{13,1},{2,6},{6,10},{... | collective-permute-start | bytes 165896 | tf_op jit(solution)/shard_map/ppermute | solution.py:361
  4.6 2.6 %collective-permute-start.4 = (bf16[24,1152]{1,0:T(8,128)(2,1)S(1)}, bf16[24,1152]{1,0:T(8,128)(2,1)S(1)}, u32[]{:S(2)}, u32[]{:S(2)}) collective-permute-start(bf16[24,1152]{1,0:T(8,128)(2,1)S(1)} %get-tuple-element.24.refs_0_), channel_id=1, source_target_pairs={{0,8},{4,12},{8,0},{12,4},{1,9},{5,13},{9,1},{13,5},{2,10},{6,14},... | collective-permute-start | bytes 165896 | tf_op jit(solution)/shard_map/ppermute | solution.py:361
  7.2 1.3 %collective-permute-start.3 = (bf16[24,1152]{1,0:T(8,128)(2,1)S(1)}, bf16[24,1152]{1,0:T(8,128)(2,1)S(1)}, u32[]{:S(2)}, u32[]{:S(2)}) collective-permute-start(bf16[24,1152]{1,0:T(8,128)(2,1)S(1)} %get-tuple-element.24.refs_0_), channel_id=1, source_target_pairs={{0,12},{4,0},{8,4},{12,8},{1,13},{5,1},{9,5},{13,9},{2,14},{6,2},{... | collective-permute-start | bytes 165896 | tf_op jit(solution)/shard_map/ppermute | solution.py:361
  8.5 0.4 %collective-permute-start = (bf16[24,1024]{1,0:T(8,128)(2,1)S(1)}, bf16[24,1024]{1,0:T(8,128)(2,1)S(1)}, u32[]{:S(2)}, u32[]{:S(2)}) collective-permute-start(bf16[24,1024]{1,0:T(8,128)(2,1)S(1)} %get-tuple-element.21), channel_id=1, source_target_pairs={{0,12},{4,0},{8,4},{12,8},{1,13},{5,1},{9,5},{13,9},{2,14},{6,2},{... | collective-permute-start | bytes 147464 | tf_op jit(solution)/shard_map/ppermute | solution.py:364
  9.0 1.7 %collective-permute-start.1 = (bf16[24,1024]{1,0:T(8,128)(2,1)S(1)}, bf16[24,1024]{1,0:T(8,128)(2,1)S(1)}, u32[]{:S(2)}, u32[]{:S(2)}) collective-permute-start(bf16[24,1024]{1,0:T(8,128)(2,1)S(1)} %get-tuple-element.22), channel_id=1, source_target_pairs={{0,8},{4,12},{8,0},{12,4},{1,9},{5,13},{9,1},{13,5},{2,10},{6,14},... | collective-permute-start | bytes 147464 | tf_op jit(solution)/shard_map/ppermute | solution.py:364
  10.7 0.0 collective-permute-done.5.refs_3_
  10.7 0.1 collective-permute-start.2
  10.7 0.2 collective-permute-done.4.refs_2_
  11.0 0.7 %collective-permute-done.3.refs_1_ = bf16[24,1152]{1,0:T(8,128)(2,1)S(1)} collective-permute-done((bf16[24,1152]{1,0:T(8,128)(2,1)S(1)}, bf16[24,1152]{1,0:T(8,128)(2,1)S(1)}, u32[]{:S(2)}, u32[]{:S(2)}) %collective-permute-start.3) | collective-permute-done | bytes 55328 | tf_op jit(solution)/shard_map/ppermute | solution.py:361
  11.7 1.9 %shard_map.120 = (f32[72,128]{1,0:T(8,128)S(1)}, f32[48,128]{1,0:T(8,128)S(1)}) custom-call(bf16[24,1152]{1,0:T(8,128)(2,1)S(1)} %get-tuple-element.24.refs_0_, bf16[24,1152]{1,0:T(8,128)(2,1)S(1)} %collective-permute-done.3.refs_1_, bf16[24,1152]{1,0:T(8,128)(2,1)S(1)} %collective-permute-done.4.refs_2_, ...), custom_call_target="tpu_custom_call" | custom-call | flops 301989888 | bytes 6291456 | tf_op jit(solution)/shard_map/pallas_call | solution.py:33
  13.5 0.1 collective-permute-start.8
  13.6 1.5 %collective-permute-start.7 = (f32[72,128]{1,0:T(8,128)S(1)}, f32[72,128]{1,0:T(8,128)S(1)}, u32[]{:S(2)}, u32[]{:S(2)}) collective-permute-start(f32[72,128]{1,0:T(8,128)S(1)} %get-tuple-element.26.refs_0_), channel_id=1, source_target_pairs={{0,2},{1,3},{2,0},{3,1},{4,6},{5,7},{6,4},{7,5},{8,10},{9,11},{10,... | collective-permute-start | bytes 110600 | tf_op jit(solution)/shard_map/ppermute | solution.py:376
  15.1 0.0 collective-permute-done.refs_1_
  15.1 0.2 collective-permute-start.6
  15.3 0.4 %collective-permute-done.1.refs_2_ = bf16[24,1024]{1,0:T(8,128)(2,1)S(1)} collective-permute-done((bf16[24,1024]{1,0:T(8,128)(2,1)S(1)}, bf16[24,1024]{1,0:T(8,128)(2,1)S(1)}, u32[]{:S(2)}, u32[]{:S(2)}) %collective-permute-start.1) | collective-permute-done | bytes 49184 | tf_op jit(solution)/shard_map/ppermute | solution.py:364
  15.7 0.8 %collective-permute-done.2.refs_3_ = bf16[24,1024]{1,0:T(8,128)(2,1)S(1)} collective-permute-done((bf16[24,1024]{1,0:T(8,128)(2,1)S(1)}, bf16[24,1024]{1,0:T(8,128)(2,1)S(1)}, u32[]{:S(2)}, u32[]{:S(2)}) %collective-permute-start.2) | collective-permute-done | bytes 49184 | tf_op jit(solution)/shard_map/ppermute | solution.py:364
  16.6 0.0 copy-start.2
  16.6 0.0 copy-start.7
  16.6 1.9 %shard_map.119.base = f32[48,2560]{1,0:T(8,128)S(1)} custom-call(bf16[24,1024]{1,0:T(8,128)(2,1)S(1)} %get-tuple-element.20.refs_0_, bf16[24,1024]{1,0:T(8,128)(2,1)S(1)} %collective-permute-done.refs_1_, bf16[24,1024]{1,0:T(8,128)(2,1)S(1)} %collective-permute-done.1.refs_2_, bf16[24,1024]{1,0:T(8,128)(2,1)S(1)} %collective-permute-done.2.refs_3_, ...), custom_call_target="tpu_custom_call" | custom-call | flops 503316480 | bytes 10485760 | tf_op jit(solution)/shard_map/pallas_call | solution.py:33
  18.5 0.0 copy-start.4
  18.5 0.0 collective-permute-done.8.refs_3_
  18.5 0.0 collective-permute-done.7.refs_2_
  18.6 0.0 copy-start.3
  18.6 0.8 %shard_map.121 = (f32[240,128]{1,0:T(8,128)S(1)}, s16[256,128]{1,0:T(8,128)(2,1)S(1)}, s16[256,128]{1,0:T(8,128)(2,1)S(1)}, s16[256,128]{1,0:T(8,128)(2,1)S(1)}) custom-call(f32[48,2560]{1,0:T(8,128)S(1)} %shard_map.119.base, f32[48,128]{1,0:T(8,128)S(1)} %get-tuple-element.25.ids, f32[72,128]{1,0:T(8,128)S(1)} %get-tuple-element.26.refs_0_, ...), custom_call_target="tpu_custom_call" | custom-call | flops 125829120 | bytes 2621440 | tf_op jit(solution)/shard_map/pallas_call | solution.py:33
  19.4 1.9 %collective-permute-start.9 = (s16[256,128]{1,0:T(8,128)(2,1)S(1)}, s16[256,128]{1,0:T(8,128)(2,1)S(1)}, u32[]{:S(2)}, u32[]{:S(2)}) collective-permute-start(s16[256,128]{1,0:T(8,128)(2,1)S(1)} %get-tuple-element.31), channel_id=1, source_target_pairs={{0,8},{4,12},{8,0},{12,4},{1,9},{5,13},{9,1},{13,5},{2,10},{6,14},... | collective-permute-start | bytes 196616 | tf_op jit(solution)/shard_map/ppermute | solution.py:402
  21.3 2.7 %collective-permute-start.10 = (s16[256,128]{1,0:T(8,128)(2,1)S(1)}, s16[256,128]{1,0:T(8,128)(2,1)S(1)}, u32[]{:S(2)}, u32[]{:S(2)}) collective-permute-start(s16[256,128]{1,0:T(8,128)(2,1)S(1)} %get-tuple-element.32), channel_id=1, source_target_pairs={{0,4},{4,8},{8,12},{12,0},{1,5},{5,9},{9,13},{13,1},{2,6},{6,10},{... | collective-permute-start | bytes 196616 | tf_op jit(solution)/shard_map/ppermute | solution.py:402
  24.0 1.1 %collective-permute-start.11 = (s16[256,128]{1,0:T(8,128)(2,1)S(1)}, s16[256,128]{1,0:T(8,128)(2,1)S(1)}, u32[]{:S(2)}, u32[]{:S(2)}) collective-permute-start(s16[256,128]{1,0:T(8,128)(2,1)S(1)} %get-tuple-element.33), channel_id=1, source_target_pairs={{0,12},{4,0},{8,4},{12,8},{1,13},{5,1},{9,5},{13,9},{2,14},{6,2},{... | collective-permute-start | bytes 196616 | tf_op jit(solution)/shard_map/ppermute | solution.py:402
  25.1 1.2 %shard_map.122 = (f32[216,128]{1,0:T(8,128)S(1)}, f32[216,128]{1,0:T(8,128)S(1)}, f32[12,192]{1,0:T(8,128)S(1)}, bf16[12,2,128,192]{3,2,1,0:T(8,128)(2,1)S(1)}) custom-call(s32[12]{0:T(128)} %lengths_far.1, f32[240,128]{1,0:T(8,128)S(1)} %get-tuple-element.27.after.refs_0_, bf16[12,2,192,128]{3,2,1,0:T(8,128)(2,1)S(1)} %copy-done.4), custom_call_target="tpu_custom_call" | custom-call | tf_op jit(solution)/shard_map/pallas_call | solution.py:33
  26.3 1.3 %collective-permute-done.10.refs_2_ = s16[256,128]{1,0:T(8,128)(2,1)S(1)} collective-permute-done((s16[256,128]{1,0:T(8,128)(2,1)S(1)}, s16[256,128]{1,0:T(8,128)(2,1)S(1)}, u32[]{:S(2)}, u32[]{:S(2)}) %collective-permute-start.10) | collective-permute-done | bytes 65568 | tf_op jit(solution)/shard_map/ppermute | solution.py:402
  27.6 0.7 %collective-permute-done.11.refs_3_ = s16[256,128]{1,0:T(8,128)(2,1)S(1)} collective-permute-done((s16[256,128]{1,0:T(8,128)(2,1)S(1)}, s16[256,128]{1,0:T(8,128)(2,1)S(1)}, u32[]{:S(2)}, u32[]{:S(2)}) %collective-permute-start.11) | collective-permute-done | bytes 65568 | tf_op jit(solution)/shard_map/ppermute | solution.py:402
  28.3 1.6 %shard_map.123 = bf16[12,2048]{1,0:T(8,128)(2,1)} custom-call(f32[12,192]{1,0:T(8,128)S(1)} %get-tuple-element.28.visible, f32[216,128]{1,0:T(8,128)S(1)} %get-tuple-element.29.cosine, f32[216,128]{1,0:T(8,128)S(1)} %get-tuple-element.30.sine, f32[240,128]{1,0:T(8,128)S(1)} %get-tuple-element.27.after.refs_0_, ...), custom_call_target="tpu_custom_call" | custom-call | flops 18874368 | bytes 2359296 | tf_op jit(solution)/shard_map/pallas_call | solution.py:33
  (14 shorter events, 0.0 us)
Async XLA Ops:
  0.0 11.7 %copy-start.1 = (bf16[8,3,64,2048]{3,2,1,0:T(8,128)(2,1)S(1)}, bf16[8,3,64,2048]{3,2,1,0:T(8,128)(2,1)}, u32[]{:S(2)}) copy-start(bf16[8,3,64,2048]{3,2,1,0:T(8,128)(2,1)} %param.21) | copy-start | bytes 18874372
  0.0 16.6 %copy-start = (bf16[2048,2048]{1,0:T(8,128)(2,1)S(1)}, bf16[2048,2048]{1,0:T(8,128)(2,1)}, u32[]{:S(2)}) copy-start(bf16[2048,2048]{1,0:T(8,128)(2,1)} %refs_4_.1) | copy-start | bytes 25165828
  1.5 9.2 %collective-permute-start.5 = (bf16[24,1152]{1,0:T(8,128)(2,1)S(1)}, bf16[24,1152]{1,0:T(8,128)(2,1)S(1)}, u32[]{:S(2)}, u32[]{:S(2)}) collective-permute-start(bf16[24,1152]{1,0:T(8,128)(2,1)S(1)} %get-tuple-element.24.refs_0_), channel_id=1, source_target_pairs={{0,4},{4,8},{8,12},{12,0},{1,5},{5,9},{9,13},{13,1},{2,6},{6,10},{... | collective-permute-start | bytes 165896 | tf_op jit(solution)/shard_map/ppermute | solution.py:361
  4.6 6.4 %collective-permute-start.4 = (bf16[24,1152]{1,0:T(8,128)(2,1)S(1)}, bf16[24,1152]{1,0:T(8,128)(2,1)S(1)}, u32[]{:S(2)}, u32[]{:S(2)}) collective-permute-start(bf16[24,1152]{1,0:T(8,128)(2,1)S(1)} %get-tuple-element.24.refs_0_), channel_id=1, source_target_pairs={{0,8},{4,12},{8,0},{12,4},{1,9},{5,13},{9,1},{13,5},{2,10},{6,14},... | collective-permute-start | bytes 165896 | tf_op jit(solution)/shard_map/ppermute | solution.py:361
  7.2 4.5 %collective-permute-start.3 = (bf16[24,1152]{1,0:T(8,128)(2,1)S(1)}, bf16[24,1152]{1,0:T(8,128)(2,1)S(1)}, u32[]{:S(2)}, u32[]{:S(2)}) collective-permute-start(bf16[24,1152]{1,0:T(8,128)(2,1)S(1)} %get-tuple-element.24.refs_0_), channel_id=1, source_target_pairs={{0,12},{4,0},{8,4},{12,8},{1,13},{5,1},{9,5},{13,9},{2,14},{6,2},{... | collective-permute-start | bytes 165896 | tf_op jit(solution)/shard_map/ppermute | solution.py:361
  8.5 6.6 %collective-permute-start = (bf16[24,1024]{1,0:T(8,128)(2,1)S(1)}, bf16[24,1024]{1,0:T(8,128)(2,1)S(1)}, u32[]{:S(2)}, u32[]{:S(2)}) collective-permute-start(bf16[24,1024]{1,0:T(8,128)(2,1)S(1)} %get-tuple-element.21), channel_id=1, source_target_pairs={{0,12},{4,0},{8,4},{12,8},{1,13},{5,1},{9,5},{13,9},{2,14},{6,2},{... | collective-permute-start | bytes 147464 | tf_op jit(solution)/shard_map/ppermute | solution.py:364
  9.0 6.8 %collective-permute-start.1 = (bf16[24,1024]{1,0:T(8,128)(2,1)S(1)}, bf16[24,1024]{1,0:T(8,128)(2,1)S(1)}, u32[]{:S(2)}, u32[]{:S(2)}) collective-permute-start(bf16[24,1024]{1,0:T(8,128)(2,1)S(1)} %get-tuple-element.22), channel_id=1, source_target_pairs={{0,8},{4,12},{8,0},{12,4},{1,9},{5,13},{9,1},{13,5},{2,10},{6,14},... | collective-permute-start | bytes 147464 | tf_op jit(solution)/shard_map/ppermute | solution.py:364
  10.7 5.9 %collective-permute-start.2 = (bf16[24,1024]{1,0:T(8,128)(2,1)S(1)}, bf16[24,1024]{1,0:T(8,128)(2,1)S(1)}, u32[]{:S(2)}, u32[]{:S(2)}) collective-permute-start(bf16[24,1024]{1,0:T(8,128)(2,1)S(1)} %get-tuple-element.23), channel_id=1, source_target_pairs={{0,4},{4,8},{8,12},{12,0},{1,5},{5,9},{9,13},{13,1},{2,6},{6,10},{... | collective-permute-start | bytes 147464 | tf_op jit(solution)/shard_map/ppermute | solution.py:364
  11.7 4.9 %copy-start.5 = (bf16[2048,256]{1,0:T(8,128)(2,1)S(1)}, bf16[2048,256]{1,0:T(8,128)(2,1)}, u32[]{:S(2)}) copy-start(bf16[2048,256]{1,0:T(8,128)(2,1)} %refs_5_.3) | copy-start | bytes 3145732
  11.7 4.9 %copy-start.6 = (bf16[2048,256]{1,0:T(8,128)(2,1)S(1)}, bf16[2048,256]{1,0:T(8,128)(2,1)}, u32[]{:S(2)}) copy-start(bf16[2048,256]{1,0:T(8,128)(2,1)} %refs_6_.1) | copy-start | bytes 3145732
  13.5 5.0 %collective-permute-start.8 = (f32[72,128]{1,0:T(8,128)S(1)}, f32[72,128]{1,0:T(8,128)S(1)}, u32[]{:S(2)}, u32[]{:S(2)}) collective-permute-start(f32[72,128]{1,0:T(8,128)S(1)} %get-tuple-element.26.refs_0_), channel_id=1, source_target_pairs={{0,3},{1,0},{2,1},{3,2},{4,7},{5,4},{6,5},{7,6},{8,11},{9,8},{10,9... | collective-permute-start | bytes 110600 | tf_op jit(solution)/shard_map/ppermute | solution.py:376
  13.6 4.9 %collective-permute-start.7 = (f32[72,128]{1,0:T(8,128)S(1)}, f32[72,128]{1,0:T(8,128)S(1)}, u32[]{:S(2)}, u32[]{:S(2)}) collective-permute-start(f32[72,128]{1,0:T(8,128)S(1)} %get-tuple-element.26.refs_0_), channel_id=1, source_target_pairs={{0,2},{1,3},{2,0},{3,1},{4,6},{5,7},{6,4},{7,5},{8,10},{9,11},{10,... | collective-permute-start | bytes 110600 | tf_op jit(solution)/shard_map/ppermute | solution.py:376
  15.1 3.4 %collective-permute-start.6 = (f32[72,128]{1,0:T(8,128)S(1)}, f32[72,128]{1,0:T(8,128)S(1)}, u32[]{:S(2)}, u32[]{:S(2)}) collective-permute-start(f32[72,128]{1,0:T(8,128)S(1)} %get-tuple-element.26.refs_0_), channel_id=1, source_target_pairs={{0,1},{1,2},{2,3},{3,0},{4,5},{5,6},{6,7},{7,4},{8,9},{9,10},{10,1... | collective-permute-start | bytes 110600 | tf_op jit(solution)/shard_map/ppermute | solution.py:376
  16.6 2.0 %copy-start.2 = (bf16[8,64,2048]{2,1,0:T(8,128)(2,1)S(1)}, bf16[8,64,2048]{2,1,0:T(8,128)(2,1)}, u32[]{:S(2)}) copy-start(bf16[8,64,2048]{2,1,0:T(8,128)(2,1)} %param.22) | copy-start | bytes 6291460
  16.6 2.0 %copy-start.7 = (bf16[8,2,64,256]{3,2,1,0:T(8,128)(2,1)S(1)}, bf16[8,2,64,256]{3,2,1,0:T(8,128)(2,1)}, u32[]{:S(2)}) copy-start(bf16[8,2,64,256]{3,2,1,0:T(8,128)(2,1)} %refs_5_.4) | copy-start | bytes 1572868
  18.5 6.6 %copy-start.4 = (bf16[12,2,192,128]{3,2,1,0:T(8,128)(2,1)S(1)}, bf16[12,2,192,128]{3,2,1,0:T(8,128)(2,1)}, u32[]{:S(2)}) copy-start(bf16[12,2,192,128]{3,2,1,0:T(8,128)(2,1)} %keys.1) | copy-start | bytes 3538948
  18.6 9.7 %copy-start.3 = (bf16[12,2,192,128]{3,2,1,0:T(8,128)(2,1)S(1)}, bf16[12,2,192,128]{3,2,1,0:T(8,128)(2,1)}, u32[]{:S(2)}) copy-start(bf16[12,2,192,128]{3,2,1,0:T(8,128)(2,1)} %refs_5_.5) | copy-start | bytes 3538948
  19.4 6.9 %collective-permute-start.9 = (s16[256,128]{1,0:T(8,128)(2,1)S(1)}, s16[256,128]{1,0:T(8,128)(2,1)S(1)}, u32[]{:S(2)}, u32[]{:S(2)}) collective-permute-start(s16[256,128]{1,0:T(8,128)(2,1)S(1)} %get-tuple-element.31), channel_id=1, source_target_pairs={{0,8},{4,12},{8,0},{12,4},{1,9},{5,13},{9,1},{13,5},{2,10},{6,14},... | collective-permute-start | bytes 196616 | tf_op jit(solution)/shard_map/ppermute | solution.py:402
  21.3 6.3 %collective-permute-start.10 = (s16[256,128]{1,0:T(8,128)(2,1)S(1)}, s16[256,128]{1,0:T(8,128)(2,1)S(1)}, u32[]{:S(2)}, u32[]{:S(2)}) collective-permute-start(s16[256,128]{1,0:T(8,128)(2,1)S(1)} %get-tuple-element.32), channel_id=1, source_target_pairs={{0,4},{4,8},{8,12},{12,0},{1,5},{5,9},{9,13},{13,1},{2,6},{6,10},{... | collective-permute-start | bytes 196616 | tf_op jit(solution)/shard_map/ppermute | solution.py:402
  24.0 4.3 %collective-permute-start.11 = (s16[256,128]{1,0:T(8,128)(2,1)S(1)}, s16[256,128]{1,0:T(8,128)(2,1)S(1)}, u32[]{:S(2)}, u32[]{:S(2)}) collective-permute-start(s16[256,128]{1,0:T(8,128)(2,1)S(1)} %get-tuple-element.33), channel_id=1, source_target_pairs={{0,12},{4,0},{8,4},{12,8},{1,13},{5,1},{9,5},{13,9},{2,14},{6,2},{... | collective-permute-start | bytes 196616 | tf_op jit(solution)/shard_map/ppermute | solution.py:402
